TPU v7x, 256 devices: a whole 4x4x8 slice. The times are simulated.
256 devices in a mesh: pool: 32 (over y, x, core), tp: 8 (over z).
Axes of the slice: x: 4, y: 4, z: 8, core: 2. Of those that a mesh axis runs over, the one named last changes fastest.
Arguments:
- attended: bfloat16 [24576, 8192], P('pool', 'tp'), may hold values from -6 to 6
- out_weight: bfloat16 [8192, 4096], P('tp'), may hold values from -0.0625 to 0.0625
- cache_down: bfloat16 [384, 64, 8192], P('pool', None, 'tp'), may hold values from -0.0625 to 0.0625
- cache_up: bfloat16 [384, 64, 4096], P('pool', None, 'tp'), may hold values from -0.75 to 0.75
- pool_down: bfloat16 [256, 64, 8192], P('pool', None, 'tp'), may hold values from -0.0625 to 0.0625
- pool_up: bfloat16 [256, 64, 4096], P('pool', None, 'tp'), may hold values from -0.75 to 0.75
- segment_rows: int32 [32, 40], P('pool'), may hold values from 1 to 48, 768 in all within a row
- missed_slots: int32 [32, 28], P('pool'), may hold values from 0 to 39, as said below
- missed_ids: int32 [32, 28], replicated, may hold values from 0 to 255, as said below
- storage: int32 [256], replicated, may hold values from 0 to 255, as said below
Outputs:
- mixed: bfloat16 [24576, 4096], P('pool', 'tp')
Inputs may be any that keep to these rules, and one draw needn't show every extreme that they name: A permutation: adapter a is kept at position storage[a], by owner storage[a] // 8 along pool. `missed_ids`: distinct adapters in each group; no owner keeps more than 2 of one group's missed adapters, and in every group some owner keeps exactly 2. `missed_slots`: distinct slots in each group, increasing. `segment_rows`: each group's entries sum to 768, the largest is 48.
All inputs are finite; a program needn't handle non-finite values.
Results may differ from a plain program's by a relative error of at most 0.0039.
Values may be sent and summed in bfloat16 or wider, within the bound.
A program may use at most 128 MiB of HBM per device.

v0:
```python
import jax
import jax.numpy as jnp
from jax import lax
from jax.sharding import PartitionSpec as P

USED = 40
MISS = 28
HITS = 12
SEG_MAX = 48


def slot_layout(lengths, row_count):
    row_ends = jnp.cumsum(lengths)
    row_starts = row_ends - lengths
    positions = jnp.arange(row_count, dtype=jnp.int32)
    row_slot = jnp.sum((positions[:, None] >= row_ends[None, :]).astype(jnp.int32), axis=1)
    within = positions - row_starts[row_slot]
    flat_index = row_slot * SEG_MAX + within
    tile_steps = jnp.arange(SEG_MAX, dtype=jnp.int32)
    source = jnp.minimum(row_starts[:, None] + tile_steps[None, :], row_count - 1)
    filled = tile_steps[None, :] < lengths[:, None]
    return (source, filled, flat_index)


def slot_order(missed):
    slots = jnp.arange(USED, dtype=jnp.int32)
    matches = missed[None, :] == slots[:, None]
    is_missed = jnp.any(matches, axis=1)
    miss_index = jnp.sum(jnp.where(matches, jnp.arange(MISS, dtype=jnp.int32)[None, :], 0), axis=1)
    hit_rank = jnp.cumsum(1 - is_missed.astype(jnp.int32)) - 1
    position = jnp.where(is_missed, HITS + miss_index, hit_rank)
    hit_match = (hit_rank[None, :] == jnp.arange(HITS, dtype=jnp.int32)[:, None]) & ~is_missed[
        None, :
    ]
    hit_list = jnp.sum(jnp.where(hit_match, slots[None, :], 0), axis=1)
    return (position, hit_list)


def routing(missed_ids, storage, per_owner):
    stored = storage[missed_ids]
    owners = stored // per_owner
    local_slot = stored % per_owner
    miss_count = missed_ids.shape[1]
    steps_in = jnp.arange(miss_count, dtype=jnp.int32)
    earlier = steps_in[None, :] < steps_in[:, None]
    same_owner = owners[:, :, None] == owners[:, None, :]
    order_rank = jnp.sum((same_owner & earlier[None, :, :]).astype(jnp.int32), axis=2)
    return (owners, local_slot, order_rank)


def owner_pick(owners, local_slot, order_rank, own_group, capacity, per_owner):
    mine_mask = owners == own_group
    slot_steps = jnp.arange(capacity, dtype=jnp.int32)
    stock_steps = jnp.arange(per_owner, dtype=jnp.int32)
    hits_slot = mine_mask[:, :, None] & (order_rank[:, :, None] == slot_steps[None, None, :])
    hits_stock = local_slot[:, :, None] == stock_steps[None, None, :]
    picked = jnp.sum(
        (hits_slot[:, :, :, None] & hits_stock[:, :, None, :]).astype(jnp.int32), axis=1
    )
    return picked.astype(jnp.bfloat16)


def per_device(
    attended,
    out_weight,
    cache_down,
    cache_up,
    pool_down,
    pool_up,
    segment_rows,
    missed_slots,
    missed_ids,
    storage,
):
    groups = lax.axis_size("pool")
    own_group = lax.axis_index("pool")
    row_count = attended.shape[0]
    rank_width = cache_down.shape[1]
    per_owner = pool_down.shape[0]
    miss_count = missed_ids.shape[1]
    capacity = (miss_count + groups - 1) // groups + 1
    partial_value = jnp.dot(attended, out_weight, preferred_element_type=jnp.float32)
    base_share = lax.psum_scatter(partial_value, "tp", scatter_dimension=1, tiled=True)
    source, filled, flat_index = slot_layout(segment_rows[0], row_count)
    missed = missed_slots[0]
    position, hit_list = slot_order(missed)
    row_tiles = attended[source] * filled[:, :, None].astype(jnp.bfloat16)
    owners, local_slot, order_rank = routing(missed_ids, storage, per_owner)
    mine_owner = lax.dynamic_index_in_dim(owners, own_group, 0, keepdims=False)
    mine_rank = lax.dynamic_index_in_dim(order_rank, own_group, 0, keepdims=False)
    flat_slot = mine_owner * capacity + mine_rank
    picked = owner_pick(owners, local_slot, order_rank, own_group, capacity, per_owner)
    absent_tile_list = row_tiles[missed]
    sent_down = jnp.einsum(
        "gka,ard->gkrd", picked, pool_down, preferred_element_type=jnp.float32
    ).astype(jnp.bfloat16)
    sent_up = jnp.einsum(
        "gka,arc->gkrc", picked, pool_up, preferred_element_type=jnp.float32
    ).astype(jnp.bfloat16)
    got_down, got_up = (
        lax.all_to_all(sent_down, "pool", split_axis=0, concat_axis=0, tiled=True),
        lax.all_to_all(sent_up, "pool", split_axis=0, concat_axis=0, tiled=True),
    )
    retrieved_down_factor = got_down.reshape((groups * capacity,) + got_down.shape[2:])[flat_slot]
    fetched_up = got_up.reshape((groups * capacity,) + got_up.shape[2:])[flat_slot]
    shrunk_miss = jnp.einsum(
        "bgu,bxu->bgx", absent_tile_list, retrieved_down_factor, preferred_element_type=jnp.float32
    )
    shrunk_hit = jnp.einsum(
        "hsd,hrd->hsr", row_tiles[hit_list], cache_down, preferred_element_type=jnp.float32
    )
    shrunk_all = jnp.concatenate([shrunk_hit, shrunk_miss], axis=0)[position]
    partial_low = shrunk_all.reshape(USED * SEG_MAX, rank_width)[flat_index]
    spread = partial_low.reshape(1, -1, 128)
    partials = lax.all_gather(spread, "tp", axis=0, tiled=True)
    summed = jnp.sum(partials, axis=0).reshape(partial_low.shape)
    shrunk_rows = summed.astype(jnp.bfloat16)
    up_fac = jnp.concatenate([cache_up, fetched_up], axis=0)[position]
    low_tiles = shrunk_rows[source] * filled[:, :, None].astype(jnp.bfloat16)
    grown_tiles = jnp.einsum("usr,urc->usc", low_tiles, up_fac, preferred_element_type=jnp.float32)
    grown = grown_tiles.reshape(USED * SEG_MAX, grown_tiles.shape[2])[flat_index]
    return (base_share + grown).astype(jnp.bfloat16)


def solution(mesh):
    return jax.shard_map(
        per_device,
        mesh=mesh,
        in_specs=(
            P("pool", "tp"),
            P("tp", None),
            P("pool", None, "tp"),
            P("pool", None, "tp"),
            P("pool", None, "tp"),
            P("pool", None, "tp"),
            P("pool", None),
            P("pool", None),
            P(),
            P(),
        ),
        out_specs=P("pool", "tp"),
        check_vma=False,
    )
```

profile of v0, /device:TPU:1, one launch (start us, length us, event | category | flops | bytes accessed | tf_op | source)
XLA Modules:
  0.0 342.2 jit_solution(2902830938673303706)
XLA Ops:
  6.6 0.9 copy.47
  7.7 5.8 %gather_fusion.3 = s32[896]{0:T(1024)S(1)} fusion(s32[256]{0:T(256)S(1)} %copy-done.2, s32[1024]{0:T(1024)S(1)} %pad_clamp_fusion.4), kind=kCustom, calls=%fused_computation.3 | custom fusion | bytes 10752 | tf_op jit(solution)/shard_map/gather | solution.py:40
  14.6 4.7 %convolution_convert_fusion = bf16[32,2,64,1024]{3,0,2,1:T(8,128)(2,1)} fusion(bf16[8,64,1024]{2,1,0:T(8,128)(2,1)S(1)} %copy-done.4, s32[32,2,8]{0,2,1:T(8,128)S(1)} %convert_reduce_fusion.1), kind=kOutput, calls=%fused_computation.11 | convolution fusion | flops 71303680 | bytes 9439232 | tf_op jit(solution)/shard_map/gka,ard->gkrd/dot_general | solution.py:94
  19.3 11.3 %copy.57 = bf16[32,2,64,1024]{3,2,1,0:T(8,128)(2,1)} copy(bf16[32,2,64,1024]{3,0,2,1:T(8,128)(2,1)} %convolution_convert_fusion) | data formatting | bytes 16777216 | tf_op jit(solution)/shard_map/convert_element_type | solution.py:96
  30.6 8.8 %all-to-all-start = ((bf16[32,2,64,1024]{3,2,1,0:T(8,128)(2,1)}), bf16[32,2,64,1024]{3,2,1,0:T(8,128)(2,1)}, u32[]{:S(2)}, u32[]{:S(2)}) async-start(bf16[32,2,64,1024]{3,2,1,0:T(8,128)(2,1)} %copy.57), calls=%async_computation.1 | async-start | bytes 16777216 | tf_op jit(solution)/shard_map/all_to_all | solution.py:101
  40.7 7.3 %gather_fusion = bf16[1920,1024]{1,0:T(8,128)(2,1)} fusion(bf16[768,1024]{1,0:T(8,128)(2,1)S(1)} %copy-done, s32[2048]{0:T(1024)S(1)} %pad_clamp_fusion), kind=kCustom, calls=%fused_computation | custom fusion | bytes 7872000 | tf_op jit(solution)/shard_map/gather | solution.py:87
  48.0 4.3 %broadcast_multiply_fusion = bf16[40,48,1024]{2,1,0:T(8,128)(2,1)} fusion(bf16[40,48,1024]{2,1,0:T(8,128)(2,1)} %bitcast.90, bf16[40,48]{1,0:T(8,128)(2,1)S(1)} %fusion.8), kind=kLoop, calls=%fused_computation.14 | loop fusion | flops 1966080 | bytes 7868160 | tf_op jit(solution)/shard_map/mul | solution.py:87
  52.4 4.4 %gather_fusion.2 = bf16[28,48,1024]{2,1,0:T(8,128)(2,1)} fusion(bf16[40,48,1024]{2,1,0:T(8,128)(2,1)} %broadcast_multiply_fusion, s32[1024]{0:T(1024)S(1)} %pad_clamp_fusion.5), kind=kCustom, calls=%fused_computation.2 | custom fusion | bytes 5505136 | tf_op jit(solution)/shard_map/gather | solution.py:93
  57.1 2.7 gather_fusion.1
  60.0 0.7 fusion.23
  60.8 4.3 %fusion.15 = (s32[768]{0:T(1024)S(1)}, s32[768,1]{0,1:T(1,128)S(1)}) fusion(s32[]{:T(128)} %bitcast.49, s32[]{:T(128)} %bitcast.50, s32[]{:T(128)} %bitcast.51, s32[]{:T(128)} %bitcast.52, s32[]{:T(128)} %bitcast.53, s32[]{:T(128)} %bitcast.55, s32[]{:T(128)} %bitcast.54, s32[768]{0:T(1024)S(1)} %convert_reduce_fusion.2), kind=kLoop, calls=%fused_computation.105 | loop fusion | flops 11520 | bytes 9244 | tf_op jit(solution)/shard_map/gather | solution.py:17
  66.8 20.4 %select_select_fusion = s32[768]{0:T(1024)S(1)} fusion(pred[768]{0:T(1024)(128)(4,1)S(1)} %get-tuple-element.39, pred[768]{0:T(1024)(128)(4,1)S(1)} %get-tuple-element.38, pred[768]{0:T(1024)(128)(4,1)S(1)} %get-tuple-element.37, pred[768]{0:T(1024)(128)(4,1)S(1)} %get-tuple-element.36, pred[768]{0:T(1024)(128)(4,1)S(1)} %get-tuple-element.35, ...), kind=kLoop, calls=%fused_computation.104 | loop fusion | flops 25344 | bytes 31620 | tf_op jit(solution)/shard_map/gather | solution.py:17
  88.5 2.7 fusion.26
  91.2 48.0 %all-to-all-done = bf16[32,2,64,1024]{3,2,1,0:T(8,128)(2,1)} async-done(((bf16[32,2,64,1024]{3,2,1,0:T(8,128)(2,1)}), bf16[32,2,64,1024]{3,2,1,0:T(8,128)(2,1)}, u32[]{:S(2)}, u32[]{:S(2)}) %all-to-all-start) | async-done | bytes 8388640 | tf_op jit(solution)/shard_map/all_to_all | solution.py:101
  139.2 6.1 %gather_fusion.4 = bf16[28,64,1024]{2,1,0:T(8,128)(2,1)} fusion(bf16[64,64,1024]{2,1,0:T(8,128)(2,1)} %bitcast.12, s32[1024]{0:T(1024)S(1)} %pad_clamp_fusion.3), kind=kCustom, calls=%fused_computation.4 | custom fusion | bytes 7340144 | tf_op jit(solution)/shard_map/gather | solution.py:104
  145.2 4.0 %fusion.27 = f32[28,48,64]{2,1,0:T(8,128)S(1)} fusion(bf16[28,48,1024]{2,1,0:T(8,128)(2,1)} %gather_fusion.2, bf16[28,64,1024]{2,1,0:T(8,128)(2,1)} %gather_fusion.4), kind=kOutput, calls=%fused_computation.123 | convolution fusion | flops 176160768 | bytes 6766592 | tf_op jit(solution)/shard_map/bgu,bxu->bgx/dot_general | solution.py:106
  150.1 1.8 gather_fusion.6
  151.9 0.8 reshape.358
  152.8 12.4 %fusion.25 = f32[768,4096]{1,0:T(8,128)} fusion(bf16[768,1024]{1,0:T(8,128)(2,1)S(1)} %copy-done, bf16[1024,4096]{1,0:T(8,128)(2,1)} %param.11), kind=kOutput, calls=%fused_computation.121 | convolution fusion | flops 6442450944 | bytes 22544384 | tf_op jit(solution)/shard_map/dot_general | solution.py:82
  165.2 1.0 copy-done.6
  166.2 1.3 convolution_convert_fusion.1
  167.5 2.4 copy.61
  169.9 60.8 %all_to_all.10 = bf16[32,2,64,512]{3,2,1,0:T(8,128)(2,1)} all-to-all(bf16[32,2,64,512]{3,2,1,0:T(8,128)(2,1)S(1)} %copy.61), channel_id=1, replica_groups=mesh['pool'=32,'tp'=8] {'pool'}, dimensions={0} | all-to-all | bytes 8388608 | tf_op jit(solution)/shard_map/all_to_all | solution.py:102
  230.8 3.2 gather_fusion.8
  233.9 1.7 pad_maximum_fusion
  235.6 4.3 %gather_fusion.9 = bf16[40,64,512]{2,1,0:T(8,128)(2,1)} fusion(bf16[40,64,512]{2,1,0:T(8,128)(2,1)} %pad_maximum_fusion, s32[1024]{0:T(1024)} %pad_clamp_fusion.2), kind=kCustom, calls=%fused_computation.9 | custom fusion | bytes 5243040 | tf_op jit(solution)/shard_map/gather | solution.py:118
  239.9 1.5 reduce_sum.65
  241.6 4.3 %gather_fusion.7 = bf16[1920,64]{1,0:T(8,128)(2,1)S(1)} fusion(bf16[768,64]{1,0:T(8,128)(2,1)S(1)} %convert_element_type.54, s32[2048]{0:T(1024)S(1)} %pad_clamp_fusion), kind=kCustom, calls=%fused_computation.7 | custom fusion | bytes 499200 | tf_op jit(solution)/shard_map/gather | solution.py:119
  245.9 4.3 %fusion.4 = f32[40,48,512]{2,1,0:T(8,128)} fusion(bf16[40,64,512]{2,1,0:T(8,128)(2,1)} %gather_fusion.9, bf16[40,48,64]{2,1,0:T(8,128)(2,1)S(1)} %bitcast.92, bf16[40,48]{1,0:T(8,128)(2,1)S(1)} %copy-done.8), kind=kOutput, calls=%fused_computation.21 | convolution fusion | flops 125952000 | bytes 6803200 | tf_op jit(solution)/shard_map/usr,urc->usc/dot_general | solution.py:120
  250.2 5.0 %gather_fusion.10 = f32[768,512]{1,0:T(8,128)S(1)} fusion(f32[1920,512]{1,0:T(8,128)} %bitcast.88, s32[1024]{0:T(1024)S(1)} %copy-done.9), kind=kCustom, calls=%fused_computation.10 | custom fusion | bytes 3148800 | tf_op jit(solution)/shard_map/gather | solution.py:121
  255.2 77.6 %reduce-scatter.2.cloned.1.call-done = f32[768,512]{1,0:T(8,128)} async-done(((f32[768,4096]{1,0:T(8,128)}), f32[768,512]{1,0:T(8,128)}) %reduce-scatter.2.cloned.1.call-update) | async-done | bytes 1572880 | tf_op jit(solution)/shard_map/reduce_scatter | solution.py:83
  332.8 2.5 add_convert_fusion
  (80 shorter events, 7.1 us)
Async XLA Ops:
  6.5 34.1 %copy-start = (bf16[768,1024]{1,0:T(8,128)(2,1)S(1)}, bf16[768,1024]{1,0:T(8,128)(2,1)}, u32[]{:S(2)}) copy-start(bf16[768,1024]{1,0:T(8,128)(2,1)} %param.10) | copy-start | bytes 4718596
  6.5 1.2 copy-start.2
  7.7 6.9 %copy-start.4 = (bf16[8,64,1024]{2,1,0:T(8,128)(2,1)S(1)}, bf16[8,64,1024]{2,1,0:T(8,128)(2,1)}, u32[]{:S(2)}) copy-start(bf16[8,64,1024]{2,1,0:T(8,128)(2,1)} %param.14) | copy-start | bytes 3145732
  30.6 9.0 %copy-start.11 = (s32[1,40]{1,0:T(1,128)S(1)}, s32[1,40]{1,0:T(1,128)}, u32[]{:S(2)}) copy-start(s32[1,40]{1,0:T(1,128)} %param.16) | copy-start | bytes 484
  30.6 9.5 %copy-start.12 = (s32[1,28]{1,0:T(1,128)S(1)}, s32[1,28]{1,0:T(1,128)}, u32[]{:S(2)}) copy-start(s32[1,28]{1,0:T(1,128)} %param.17) | copy-start | bytes 340
  30.6 108.5 %all-to-all-start = ((bf16[32,2,64,1024]{3,2,1,0:T(8,128)(2,1)}), bf16[32,2,64,1024]{3,2,1,0:T(8,128)(2,1)}, u32[]{:S(2)}, u32[]{:S(2)}) async-start(bf16[32,2,64,1024]{3,2,1,0:T(8,128)(2,1)} %copy.57), calls=%async_computation.1 | async-start | bytes 16777216 | tf_op jit(solution)/shard_map/all_to_all | solution.py:101
  39.4 200.5 %all-gather.2.cloned.1.call-start = ((), (), s32[]{:S(2)}) async-start(), calls=%async_computation.4 | async-start | bytes 1769472 | tf_op jit(solution)/shard_map/all_gather | solution.py:115
  48.0 4.3 %copy-start.7 = (bf16[40,48]{1,0:T(8,128)(2,1)}, bf16[40,48]{1,0:T(8,128)(2,1)S(1)}, u32[]{:S(2)}) copy-start(bf16[40,48]{1,0:T(8,128)(2,1)S(1)} %fusion.8) | copy-start | bytes 11524
  87.9 57.4 %copy-start.10 = (s32[1024]{0:T(1024)}, s32[1024]{0:T(1024)S(1)}, u32[]{:S(2)}) copy-start(s32[1024]{0:T(1024)S(1)} %pad_clamp_fusion.3) | copy-start | bytes 12292
  145.2 4.0 %copy-start.3 = (f32[12,48,64]{2,1,0:T(8,128)S(1)}, f32[12,48,64]{2,1,0:T(8,128)}, u32[]{:S(2)}) copy-start(f32[12,48,64]{2,1,0:T(8,128)} %fusion.26) | copy-start | bytes 442372
  152.8 180.1 %reduce-scatter.2.cloned.1.call-start = ((), (), s32[]{:S(2)}) async-start(), calls=%async_computation.3 | async-start | bytes 14155776 | tf_op jit(solution)/shard_map/reduce_scatter | solution.py:83
  165.2 1.0 copy-start.6
  230.8 3.2 copy-start.5
  241.4 4.4 %copy-start.8 = (bf16[40,48]{1,0:T(8,128)(2,1)S(1)}, bf16[40,48]{1,0:T(8,128)(2,1)}, u32[]{:S(2)}) copy-start(bf16[40,48]{1,0:T(8,128)(2,1)} %copy-done.7) | copy-start | bytes 11524
  245.9 4.3 %copy-start.9 = (s32[1024]{0:T(1024)S(1)}, s32[1024]{0:T(1024)}, u32[]{:S(2)}) copy-start(s32[1024]{0:T(1024)} %pad_clamp_fusion.1) | copy-start | bytes 12292
  250.2 85.1 %copy-start.1 = (bf16[768,1024]{1,0:T(8,128)(2,1)S(1)}, bf16[768,1024]{1,0:T(8,128)(2,1)}, u32[]{:S(2)}) copy-start(bf16[768,1024]{1,0:T(8,128)(2,1)} %param.10) | copy-start | bytes 4718596
Sparse Core Ops, SparseCore 0:
  152.9 40.2 all-gather.1
  195.7 137.0 reduce-scatter.1
where the time goes:
time: 343 us; the launch traced here: 342 us
  waiting for transfers between devices  126 us (37%)
  local copies, waits for them, and re-layouts  65.2 us (19%)
  blocking collectives  60.8 us (18%)
  other arithmetic  38.4 us (11%)
  matrix products  29.4 us (9%)
  between operations  13.7 us (4%)
  starting transfers between devices  9.05 us (3%)
    reduce_scatter x1, waiting for transfers between devices, per_device(): lax.psum_scatter(partial_value, 'tp', scatter_dimension=1, tiled=True)  77.6 us
    all_to_all x1, blocking collectives, per_device(): lax.all_to_all(sent_up, 'pool', split_axis=0, concat_axis=0, tiled=True)  60.8 us
    all_to_all x1, waiting for transfers between devices, per_device(): lax.all_to_all(sent_down, 'pool', split_axis=0, concat_axis=0, tiled=True)  48 us
    gather x3, other arithmetic, slot_layout(): within = positions - row_starts[row_slot]  25 us
    dot_general x1, matrix products, per_device(): jnp.dot(attended, out_weight, preferred_element_type=jnp.float32)  12.4 us
    convert_element_type x1, local copies, waits for them, and re-layouts, per_device(): sent_down = jnp.einsum('gka,ard->gkrd', picked, pool_down, preferred_elem...  11.3 us
    all_to_all x1, starting transfers between devices, per_device(): lax.all_to_all(sent_down, 'pool', split_axis=0, concat_axis=0, tiled=True)  8.79 us
    gather x1, local copies, waits for them, and re-layouts, per_device(): row_tiles = attended[source] * filled[:, :, None].astype(jnp.bfloat16)  7.26 us
  transfers between devices with their start and end apart: 3, of which 2 were waited for; matrix products, arithmetic and copies ran while one was open for 27% of the time, Pallas kernels for 0%

commit v1 on v0

v1 whole, which is shorter than its diff:
```python
import functools

import jax
import jax.numpy as jnp
from jax import lax
from jax.experimental import pallas as pl
from jax.experimental.pallas import tpu as pltpu
from jax.sharding import PartitionSpec as P

USED = 40
MISS = 28
HITS = 12
ROWS = 768
KD = 1024
CHUNK = 512
HALF = 256
NZ = 8
BF = jnp.bfloat16
F32 = jnp.float32
MESH = pl.DeviceIdType.MESH
NT = (((1,), (1,)), ((), ()))


def kernel(
    att_h, w_h, cd_h, cu_h, pd_h, pu_h, seg, mslots, mids, stor,
    out_ref,
    att, w, cd, cu, sd, su, dd, du, rd, ru, zr, zs, base, prow, part, ar, own_sh, sh, sexp,
    pos, slot_s,
    in_sem, loc_sem, p1_s, p1_r, g_s, g_r, d_s, d_r, z_s, z_r, a_s, a_r,
):
    p = lax.axis_index("pool")
    z = lax.axis_index("tp")
    y, x, c = p // 8, (p // 2) % 4, p % 2
    member = (x * 2 + c, y * 2 + c)
    ring = (y, x)

    def device(mode, q):
        return y * 8 + q if mode == 0 else (q // 2) * 8 + x * 2 + q % 2

    def ring_next(mode, step):
        if mode == 0:
            return ((y + step) % 4) * 8 + x * 2 + c
        return y * 8 + ((x + step) % 4) * 2 + c

    def remote(src, dst, ss, rs, pool, tp):
        return pltpu.make_async_remote_copy(
            src_ref=src, dst_ref=dst, send_sem=ss, recv_sem=rs,
            device_id=(pool, tp), device_id_type=MESH,
        )

    sends = []

    loads = {}
    loads["att"] = pltpu.make_async_copy(att_h, att, in_sem.at[8])
    loads["cd"] = pltpu.make_async_copy(cd_h, cd, in_sem.at[9])
    loads["cu"] = pltpu.make_async_copy(cu_h, cu, in_sem.at[10])
    for k in range(NZ):
        d = (z + k) % NZ
        loads[k] = pltpu.make_async_copy(
            w_h.at[:, pl.ds(pl.multiple_of(d * CHUNK, CHUNK), CHUNK)], w.at[k], in_sem.at[k]
        )
    for k in ("att", 4, 3, 5, 2, 6, 1, 7, 0, "cd", "cu"):
        loads[k].start()

    bar = pltpu.get_barrier_semaphore()
    for mode in range(2):
        for o in range(1, 8):
            pl.semaphore_signal(
                bar, inc=1, device_id=(device(mode, (member[mode] + o) % 8), z), device_id_type=MESH
            )
    for o in range(1, NZ):
        pl.semaphore_signal(bar, inc=1, device_id=(p, (z + o) % NZ), device_id_type=MESH)
    pl.semaphore_wait(bar, 21)

    def spread_src(kind, mode, q):
        if kind == 0:
            return pd_h.at[:, pl.ds(32 * mode, 32), pl.ds(pl.multiple_of(q * 128, 128), 128)]
        return pu_h.at[
            :,
            pl.ds(pl.multiple_of(32 * mode + 16 * (q // 4), 16), 16),
            pl.ds(pl.multiple_of((q % 4) * 128, 128), 128),
        ]

    stock = (sd, su)

    def spread_dst(kind, mode, q):
        return stock[kind].at[mode, pl.ds(ring[mode] * 64 + q * 8, 8)]

    own_spread = {}

    def spread_start(kind):
        for o in (1, 7, 2, 6, 3, 5, 4):
            for mode in range(2):
                q = member[mode]
                t = (q + o) % 8
                cp = remote(
                    spread_src(kind, mode, t), spread_dst(kind, mode, q),
                    p1_s.at[mode, kind, o - 1], p1_r.at[mode, kind, o - 1], device(mode, t), z,
                )
                cp.start()
                sends.append(cp)
        for mode in range(2):
            q = member[mode]
            cp = pltpu.make_async_copy(
                spread_src(kind, mode, q), spread_dst(kind, mode, q), loc_sem.at[mode, kind]
            )
            cp.start()
            own_spread[mode, kind] = cp

    def spread_wait(kind, mode):
        q = member[mode]
        own_spread[mode, kind].wait()
        for o in range(1, 8):
            f = (q + 8 - o) % 8
            remote(
                spread_dst(kind, mode, f), spread_dst(kind, mode, f),
                p1_s.at[mode, kind, o - 1], p1_r.at[mode, kind, o - 1], device(mode, f), z,
            ).wait_recv()

    def shard(kind, mode, r, first, count):
        return stock[kind].at[mode, pl.ds(((ring[mode] + r) % 4) * 64 + first, count)]

    def gather_copy(kind, mode, i, ref):
        step = 1 if i % 2 == 0 else 3
        return remote(
            ref, ref, g_s.at[mode, kind, i], g_r.at[mode, kind, i], ring_next(mode, step), z
        )

    def gather_start(kind, mode):
        for i in range(2):
            cp = gather_copy(kind, mode, i, shard(kind, mode, 0, 0, 64))
            cp.start()
            sends.append(cp)

    def gather_forward(kind, mode):
        for i in range(2):
            r = 3 if i == 0 else 1
            got = shard(kind, mode, r, 0, 64)
            gather_copy(kind, mode, i, got).wait_recv()
            cp = gather_copy(kind, mode, 2 + i, shard(kind, mode, r, 32 * i, 32))
            cp.start()
            sends.append(cp)

    def gather_wait(kind, mode):
        for i in range(2):
            gather_copy(kind, mode, 2 + i, shard(kind, mode, 2, 32 * i, 32)).wait_recv()

    staged = (dd, du)
    got = (rd, ru)
    own_deliver = {}

    def positions():
        for mode in range(2):
            for q in range(8):
                g = device(mode, q)

                def one(j, carry, mode=mode, q=q, g=g):
                    s = stor[mids[g, j]]
                    if mode == 1:
                        s = ((s // 16) % 4) * 64 + (s // 64) * 16 + s % 16
                    pos[mode * 8 + q, j] = s
                    return carry

                lax.fori_loop(0, MISS, one, 0, unroll=4)

    def select(kind, mode, t, o):
        def one(j, carry):
            at = pos[mode * 8 + t, j]
            staged[kind][mode, o, j] = stock[kind][mode, at]
            return carry

        lax.fori_loop(0, MISS, one, 0, unroll=4)

    def deliver(kind):
        for o in (1, 7, 2, 6, 3, 5, 4, 0):
            for mode in range(2):
                q = member[mode]
                t = (q + o) % 8
                select(kind, mode, t, o)
                if o:
                    cp = remote(
                        staged[kind].at[mode, o], got[kind].at[mode, q],
                        d_s.at[mode, kind, o - 1], d_r.at[mode, kind, o - 1], device(mode, t), z,
                    )
                    cp.start()
                    sends.append(cp)
                else:
                    cp = pltpu.make_async_copy(
                        staged[kind].at[mode, o], got[kind].at[mode, q], loc_sem.at[mode, 2 + kind]
                    )
                    cp.start()
                    own_deliver[mode, kind] = cp

    def deliver_wait(kind, mode):
        q = member[mode]
        own_deliver[mode, kind].wait()
        for o in range(1, 8):
            f = (q + 8 - o) % 8
            remote(
                staged[kind].at[mode, o], got[kind].at[mode, f],
                d_s.at[mode, kind, o - 1], d_r.at[mode, kind, o - 1], device(mode, f), z,
            ).wait_recv()

    def ring_copy(way, k):
        to = (z + 1) % NZ if way == 0 else (z + NZ - 1) % NZ
        return remote(zs.at[way, k], zr.at[way, k], z_s.at[way, k], z_r.at[way, k], p, to)

    def ring_step(k):
        for way in range(2):
            dist = 4 - (k + 1) // 2
            d = dist if way == 0 else NZ - dist
            half = (k + way) % 2
            if k >= 2:
                ring_copy(way, k - 2).wait_recv()

            def tile(i, carry, d=d, half=half, way=way):
                rows = pl.ds(pl.multiple_of(i * 256, 256), 256)
                v = jnp.dot(
                    att[rows, :], w[d, :, HALF * half:HALF * half + HALF],
                    preferred_element_type=F32,
                )
                if k >= 2:
                    v = v + zr[way, k - 2, rows, :].astype(F32)
                zs[way, k, rows, :] = v.astype(BF)
                return carry

            lax.fori_loop(0, 3, tile, 0)
            cp = ring_copy(way, k)
            cp.start()
            sends.append(cp)

    def own_chunk():
        loads[0].wait()

        def tile(i, carry):
            rows = pl.ds(pl.multiple_of(i * 256, 256), 256)
            for half in range(2):
                cols = slice(HALF * half, HALF * half + HALF)
                base[rows, cols] = jnp.dot(
                    att[rows, :], w[0, :, cols], preferred_element_type=F32
                )
            return carry

        lax.fori_loop(0, 3, tile, 0)

    def row_positions():
        def one(s, carry):
            start, missed, hit = carry
            is_miss = jnp.logical_and(missed < MISS, mslots[0, jnp.minimum(missed, MISS - 1)] == s)
            slot_s[0, s] = start
            slot_s[1, s] = jnp.where(is_miss, HITS + missed, hit)
            step = jnp.where(is_miss, 1, 0)
            return start + seg[0, s], missed + step, hit + 1 - step

        lax.fori_loop(0, USED, one, (jnp.int32(0), jnp.int32(0), jnp.int32(0)))

        def tile(i, carry):
            rows = i * 96 + lax.broadcasted_iota(jnp.int32, (96, 128), 0)

            def slot(s, v):
                return jnp.where(rows >= slot_s[0, s], slot_s[1, s], v)

            prow[pl.ds(pl.multiple_of(i * 96, 96), 96), :] = lax.fori_loop(
                0, USED, slot, jnp.zeros((96, 128), jnp.int32), unroll=8
            )
            return carry

        lax.fori_loop(0, 8, tile, 0)

    def shrink():
        lane = lax.broadcasted_iota(jnp.int32, (384, 128), 1)
        packed = []
        for t in range(2):
            rows = slice(384 * t, 384 * t + 384)
            pm = prow[rows, :] - lane // 32
            a = att[rows, :]
            sums = []
            for mode in range(2):
                hit = cd[:, 32 * mode:32 * mode + 32, :].reshape(HITS * 32, KD)
                xh = lax.dot_general(a, hit, NT, preferred_element_type=F32)
                acc = jnp.zeros((384, 128), F32)
                for b in range(3):
                    acc = acc + jnp.where(pm == 4 * b, xh[:, 128 * b:128 * b + 128], 0.0)
                miss = jnp.concatenate(
                    [rd[mode, q].reshape(MISS * 32, 128) for q in range(8)], axis=1
                )
                xm = lax.dot_general(a, miss, NT, preferred_element_type=F32)
                for b in range(7):
                    acc = acc + jnp.where(
                        pm == HITS + 4 * b, xm[:, 128 * b:128 * b + 128], 0.0
                    )
                acc = acc + pltpu.roll(acc, 64, 1)
                acc = acc + pltpu.roll(acc, 32, 1)
                sums.append(acc)
            packed.append(jnp.where((lane // 32) % 2 == 0, sums[0], sums[1]))
        part[...] = jnp.where(lane < 64, packed[0], packed[1])

    def scatter_copy(o):
        t = (z + o) % NZ
        return remote(
            part.at[pl.ds(pl.multiple_of(t * 48, 16), 48)], ar.at[o - 1],
            a_s.at[0, o - 1], a_r.at[0, o - 1], p, t,
        )

    def ranks_copy(o, src):
        t = (z + o) % NZ
        dst = sh.at[pl.ds(pl.multiple_of(src * 48, 16), 48)]
        return remote(own_sh, dst, a_s.at[1, o - 1], a_r.at[1, o - 1], p, t)

    def own_ranks_copy():
        return pltpu.make_async_copy(
            own_sh, sh.at[pl.ds(pl.multiple_of(z * 48, 16), 48)], in_sem.at[11]
        )

    def rank_sums():
        order = (4, 3, 5, 2, 6, 1, 7)
        for o in order:
            cp = scatter_copy(o)
            cp.start()
            sends.append(cp)
        mine = pl.ds(pl.multiple_of(z * 48, 16), 48)
        total = part[mine, :]
        for o in (1, 7, 2, 6, 3, 5, 4):
            scatter_copy(o).wait_recv()
        for o in range(7):
            total = total + ar[o]
        own_sh[...] = total.astype(BF)
        own_ranks_copy().start()
        for o in order:
            cp = ranks_copy(o, z)
            cp.start()
            sends.append(cp)

    def ranks_wait():
        own_ranks_copy().wait()
        for o in (1, 7, 2, 6, 3, 5, 4):
            ranks_copy(o, (z + NZ - o) % NZ).wait_recv()

    def expand():
        lane = lax.broadcasted_iota(jnp.int32, (384, 128), 1)
        row_e = lax.broadcasted_iota(jnp.int32, (128, 512), 0)
        col_e = lax.broadcasted_iota(jnp.int32, (128, 512), 1)
        s = sh[...]
        for t in range(2):
            rows = slice(384 * t, 384 * t + 384)
            pick = row_e == 64 * t + (col_e // 128) * 16 + col_e % 16
            spread = jnp.dot(s, jnp.where(pick, 1.0, 0.0).astype(BF), preferred_element_type=F32)
            pm = prow[rows, :] - lane // 16
            for b in range(5):
                m = pm == 8 * b
                for rb in range(4):
                    sexp[rows, 640 * rb + 128 * b:640 * rb + 128 * b + 128] = jnp.where(
                        m, spread[:, 128 * rb:128 * rb + 128], 0.0
                    ).astype(BF)

    def grow():
        for rb in range(4):
            mode, first = rb // 2, (rb % 2) * 4
            up = jnp.concatenate(
                [
                    cu[:, 16 * rb:16 * rb + 16, :].reshape(HITS * 16, CHUNK),
                    jnp.concatenate(
                        [ru[mode, first + cb].reshape(MISS * 16, 128) for cb in range(4)], axis=1
                    ),
                ],
                axis=0,
            )
            for t in range(2):
                rows = slice(384 * t, 384 * t + 384)
                base[rows, :] += jnp.dot(
                    sexp[rows, 640 * rb:640 * rb + 640], up, preferred_element_type=F32
                )

    def finish():
        for way in range(2):
            for k in (5, 6):
                ring_copy(way, k).wait_recv()
        for half in range(2):
            cols = slice(HALF * half, HALF * half + HALF)
            k0 = 6 if half == 0 else 5
            out_ref[:, cols] = (
                base[:, cols]
                + zr[0, k0].astype(F32)
                + zr[1, 11 - k0].astype(F32)
            ).astype(BF)

    spread_start(0)
    loads["att"].wait()
    loads[4].wait()
    ring_step(0)
    spread_start(1)
    loads[3].wait()
    loads[5].wait()
    ring_step(1)
    positions()
    row_positions()
    for mode in range(2):
        spread_wait(0, mode)
        gather_start(0, mode)
    ring_step(2)
    for mode in range(2):
        spread_wait(1, mode)
        gather_start(1, mode)
    loads[2].wait()
    loads[6].wait()
    ring_step(3)
    for mode in range(2):
        gather_forward(0, mode)
    ring_step(4)
    for mode in range(2):
        gather_forward(1, mode)
    loads[1].wait()
    loads[7].wait()
    for mode in range(2):
        gather_wait(0, mode)
    deliver(0)
    ring_step(5)
    for mode in range(2):
        gather_wait(1, mode)
    deliver(1)
    ring_step(6)
    own_chunk()
    loads["cd"].wait()
    loads["cu"].wait()
    for mode in range(2):
        deliver_wait(0, mode)
    shrink()
    rank_sums()
    ranks_wait()
    expand()
    for mode in range(2):
        deliver_wait(1, mode)
    grow()
    finish()
    for cp in sends:
        cp.wait_send()


def per_device(*args):
    hbm = pl.BlockSpec(memory_space=pl.ANY)
    smem = pl.BlockSpec(memory_space=pltpu.SMEM)
    dma = pltpu.SemaphoreType.DMA
    return pl.pallas_call(
        kernel,
        out_shape=jax.ShapeDtypeStruct((ROWS, CHUNK), BF),
        in_specs=[hbm] * 6 + [smem] * 4,
        out_specs=pl.BlockSpec(memory_space=pltpu.VMEM),
        scratch_shapes=[
            pltpu.VMEM((ROWS, KD), BF),
            pltpu.VMEM((NZ, KD, CHUNK), BF),
            pltpu.VMEM((HITS, 64, KD), BF),
            pltpu.VMEM((HITS, 64, CHUNK), BF),
            pltpu.VMEM((2, 256, 32, 128), BF),
            pltpu.VMEM((2, 256, 16, 128), BF),
            pltpu.VMEM((2, 8, MISS, 32, 128), BF),
            pltpu.VMEM((2, 8, MISS, 16, 128), BF),
            pltpu.VMEM((2, 8, MISS, 32, 128), BF),
            pltpu.VMEM((2, 8, MISS, 16, 128), BF),
            pltpu.VMEM((2, 7, ROWS, HALF), BF),
            pltpu.VMEM((2, 7, ROWS, HALF), BF),
            pltpu.VMEM((ROWS, CHUNK), F32),
            pltpu.VMEM((ROWS, 128), jnp.int32),
            pltpu.VMEM((384, 128), F32),
            pltpu.VMEM((7, 48, 128), F32),
            pltpu.VMEM((48, 128), BF),
            pltpu.VMEM((384, 128), BF),
            pltpu.VMEM((ROWS, 2560), BF),
            pltpu.SMEM((16, MISS), jnp.int32),
            pltpu.SMEM((2, USED), jnp.int32),
            dma((12,)),
            dma((2, 4)),
            dma((2, 2, 7)),
            dma((2, 2, 7)),
            dma((2, 2, 4)),
            dma((2, 2, 4)),
            dma((2, 2, 7)),
            dma((2, 2, 7)),
            dma((2, 7)),
            dma((2, 7)),
            dma((2, 7)),
            dma((2, 7)),
        ],
        compiler_params=pltpu.CompilerParams(
            collective_id=0, has_side_effects=True, vmem_limit_bytes=60 * 1024 * 1024
        ),
        cost_estimate=pl.CostEstimate(
            flops=12_500_000_000, bytes_accessed=14_000_000, transcendentals=0
        ),
        name="lora_projection",
    )(*args)


def solution(mesh):
    return jax.shard_map(
        per_device,
        mesh=mesh,
        in_specs=(
            P("pool", "tp"),
            P("tp", None),
            P("pool", None, "tp"),
            P("pool", None, "tp"),
            P("pool", None, "tp"),
            P("pool", None, "tp"),
            P("pool", None),
            P("pool", None),
            P(),
            P(),
        ),
        out_specs=P("pool", "tp"),
        check_vma=False,
    )
```

time: 343 us -> 94.7 us (0.28)
  waiting for transfers between devices: 126 us -> 0 us
  Pallas kernels: 0 us -> 91.9 us
  local copies, waits for them, and re-layouts: 65.2 us -> 2.06 us
  blocking collectives: 60.8 us -> 0 us
  other arithmetic: 38.4 us -> 0 us
  matrix products: 29.4 us -> 0 us
  between operations: 13.7 us -> 0.01 us
  starting transfers between devices: 9.05 us -> 0 us
    pallas_call x0 -> x1, Pallas kernels: none -> 91.9 us  [per_device(): pl.pallas_call(kernel, out_shape=jax.ShapeDtypeStruct((ROWS, CHUNK), BF),...]
    reduce_scatter x1 -> x0, waiting for transfers between devices: 77.6 us -> none  [per_device(): lax.psum_scatter(partial_value, 'tp', scatter_dimension=1, tiled=True)]
    all_to_all x1 -> x0, blocking collectives: 60.8 us -> none  [per_device(): lax.all_to_all(sent_up, 'pool', split_axis=0, concat_axis=0, tiled=True)]
    all_to_all x1 -> x0, waiting for transfers between devices: 48 us -> none  [per_device(): lax.all_to_all(sent_down, 'pool', split_axis=0, concat_axis=0, tiled=True)]
    gather x16 -> x0, local copies, waits for them, and re-layouts: 47.9 us -> none  [the longest x1 7.26 us: per_device(): row_tiles = attended[source] * filled[:, :, None].astype(jnp.bfloat16)]
    dot_general x6 -> x0, matrix products: 29.4 us -> none  [the longest x1 12.4 us: per_device(): jnp.dot(attended, out_weight, preferred_element_type=jnp.float32)]
    gather x10 -> x0, other arithmetic: 26.2 us -> none  [the longest x3 25 us: slot_layout(): within = positions - row_starts[row_slot]]
    convert_element_type x3 -> x0, local copies, waits for them, and re-layouts: 13.8 us -> none  [the longest x1 11.3 us: per_device(): sent_down = jnp.einsum('gka,ard->gkrd', picked, pool_down, preferred_elem...]
  transfers between devices with their start and end apart: 3 -> 0, of which waited for: 2 -> 0; matrix products, arithmetic and copies ran while one was open for 27% -> 0% of each run, Pallas kernels for 0% -> 0%
where the time goes in v1:
time: 94.7 us; the launch traced here: 94 us
  Pallas kernels  91.9 us (97%)
  local copies, waits for them, and re-layouts  2.06 us (2%)
    pallas_call x1, Pallas kernels, per_device(): pl.pallas_call(kernel, out_shape=jax.ShapeDtypeStruct((ROWS, CHUNK), BF),...  91.9 us
    unnamed x1, local copies, waits for them, and re-layouts  2.06 us

profile of v1, /device:TPU:1, one launch (start us, length us, event | category | flops | bytes accessed | tf_op | source)
XLA Modules:
  0.0 94.0 jit_solution(1113349516205708697)
XLA Ops:
  0.0 91.9 %lora_projection.1 = bf16[768,512]{1,0:T(8,128)(2,1)} custom-call(bf16[768,1024]{1,0:T(8,128)(2,1)} %att_h.1, bf16[1024,4096]{1,0:T(8,128)(2,1)} %w_h.1, bf16[12,64,1024]{2,1,0:T(8,128)(2,1)} %cd_h.1, bf16[12,64,512]{2,1,0:T(8,128)(2,1)} %cu_h.1, bf16[8,64,1024]{2,1,0:T(8,128)(2,1)} %pd_h.1, bf16[8,64,512]{2,1,0:T(8,128)(2,1)} %pu_h.1, s32[1,40]{1,0:T(1,128)} %seg.1, ...), custom_call_target="tpu_custom_call" | custom-call | flops 12499999744 | bytes 14000000 | tf_op jit(solution)/shard_map/lora_projection/pallas_call | solution.py:443
  91.9 2.1 %copy.12 = bf16[768,512]{1,0:T(8,128)(2,1)} copy(bf16[768,512]{1,0:T(8,128)(2,1)} %lora_projection.1) | data formatting | bytes 1572864

commit v2 on v1

v2 whole, which is shorter than its diff:
```python
import functools

import jax
import jax.numpy as jnp
from jax import lax
from jax.experimental import pallas as pl
from jax.experimental.pallas import tpu as pltpu
from jax.sharding import PartitionSpec as P

USED = 40
MISS = 28
HITS = 12
ROWS = 768
KD = 1024
CHUNK = 512
HALF = 256
NZ = 8
BF = jnp.bfloat16
F32 = jnp.float32
MESH = pl.DeviceIdType.MESH
NT = (((1,), (1,)), ((), ()))


def kernel(
    att_h, w_h, cd_h, cu_h, pd_h, pu_h, seg_h, mslots_h, mids_h, stor_h,
    out_ref,
    att, w, cd, cu, pd, pu, sd, su, dd, du, rd, ru, zr, zs, base, prow, hacc, part, ar, own_sh, sh, sexp,
    seg, mslots, mids, stor, pos, slot_s,
    in_sem, loc_sem, p1_s, p1_r, g_s, g_r, d_s, d_r, z_s, z_r, a_s, a_r,
):
    p = lax.axis_index("pool")
    z = lax.axis_index("tp")
    y, x, c = p // 8, (p // 2) % 4, p % 2
    member = (x * 2 + c, y * 2 + c)
    ring = (y, x)

    def device(mode, q):
        return y * 8 + q if mode == 0 else (q // 2) * 8 + x * 2 + q % 2

    def ring_next(mode, step):
        if mode == 0:
            return ((y + step) % 4) * 8 + x * 2 + c
        return y * 8 + ((x + step) % 4) * 2 + c

    def remote(src, dst, ss, rs, pool, tp):
        return pltpu.make_async_remote_copy(
            src_ref=src, dst_ref=dst, send_sem=ss, recv_sem=rs,
            device_id=(pool, tp), device_id_type=MESH,
        )

    def partner(mode, e, back=False):
        place = (member[mode] // 2 + (4 - e // 2 if back else e // 2)) % 4
        return place * 2 + (c + e) % 2

    near_last = (4, 5, 2, 6, 3, 7, 1)
    sends = []

    bar = pltpu.get_barrier_semaphore()
    for mode in range(2):
        for o in range(1, 8):
            pl.semaphore_signal(
                bar, inc=1, device_id=(device(mode, partner(mode, o)), z), device_id_type=MESH
            )
    for o in range(1, NZ):
        pl.semaphore_signal(bar, inc=1, device_id=(p, (z + o) % NZ), device_id_type=MESH)

    loads = {}
    loads["att"] = pltpu.make_async_copy(att_h, att, in_sem.at[8])
    loads["cd"] = pltpu.make_async_copy(cd_h, cd, in_sem.at[9])
    loads["cu"] = pltpu.make_async_copy(cu_h, cu, in_sem.at[10])
    loads["pd"] = pltpu.make_async_copy(pd_h, pd, in_sem.at[12])
    loads["pu"] = pltpu.make_async_copy(pu_h, pu, in_sem.at[13])
    for k, (src, dst) in enumerate(
        ((seg_h, seg), (mslots_h, mslots), (mids_h, mids), (stor_h, stor))
    ):
        loads["int", k] = pltpu.make_async_copy(src, dst, in_sem.at[17 + k])
    for k in range(NZ):
        d = (z + k) % NZ
        loads[k] = pltpu.make_async_copy(
            w_h.at[:, pl.ds(pl.multiple_of(d * CHUNK, CHUNK), CHUNK)], w.at[k], in_sem.at[k]
        )
    for k in ("pd", "pu", "att", 4, 3, 5):
        loads[k].start()
    for k in range(4):
        loads["int", k].start()
    for k in (2, 6, 1, 7, 0, "cd", "cu"):
        loads[k].start()
    pl.semaphore_wait(bar, 21)

    def spread_src(kind, mode, q):
        if kind == 0:
            return pd.at[:, pl.ds(32 * mode, 32), pl.ds(pl.multiple_of(q * 128, 128), 128)]
        return pu.at[
            :,
            pl.ds(pl.multiple_of(32 * mode + 16 * (q // 4), 16), 16),
            pl.ds(pl.multiple_of((q % 4) * 128, 128), 128),
        ]

    stock = (sd, su)

    def spread_dst(kind, mode, q):
        return stock[kind].at[mode, pl.ds(ring[mode] * 64 + q * 8, 8)]

    own_spread = {}

    def spread_start(kind):
        for o in near_last:
            for mode in range(2):
                q = member[mode]
                t = partner(mode, o)
                cp = remote(
                    spread_src(kind, mode, t), spread_dst(kind, mode, q),
                    p1_s.at[mode, kind, o - 1], p1_r.at[mode, kind, o - 1], device(mode, t), z,
                )
                cp.start()
                sends.append(cp)
        for mode in range(2):
            q = member[mode]
            cp = pltpu.make_async_copy(
                spread_src(kind, mode, q), spread_dst(kind, mode, q), loc_sem.at[mode, kind]
            )
            cp.start()
            own_spread[mode, kind] = cp

    def spread_wait(kind, mode):
        q = member[mode]
        own_spread[mode, kind].wait()
        for o in range(1, 8):
            f = partner(mode, o, True)
            remote(
                spread_dst(kind, mode, f), spread_dst(kind, mode, f),
                p1_s.at[mode, kind, o - 1], p1_r.at[mode, kind, o - 1], device(mode, f), z,
            ).wait_recv()

    def shard(kind, mode, r, first, count):
        return stock[kind].at[mode, pl.ds(((ring[mode] + r) % 4) * 64 + first, count)]

    def gather_copy(kind, mode, i, ref):
        step = 1 if i % 2 == 0 else 3
        return remote(
            ref, ref, g_s.at[mode, kind, i], g_r.at[mode, kind, i], ring_next(mode, step), z
        )

    halves = ((0, 0), (0, 32), (0, 32), (0, 0), (3, 0), (1, 32))

    def gather_send(kind, mode, i):
        r, first = halves[i]
        cp = gather_copy(kind, mode, i, shard(kind, mode, r, first, 32))
        cp.start()
        sends.append(cp)

    def gather_recv(kind, mode, i):
        r, first = halves[i]
        r = (r + (3 if i % 2 == 0 else 1)) % 4
        gather_copy(kind, mode, i, shard(kind, mode, r, first, 32)).wait_recv()

    def gather_start(kind, mode):
        for i in range(4):
            gather_send(kind, mode, i)

    def gather_forward(kind, mode):
        for i in range(2):
            gather_recv(kind, mode, i)
            gather_send(kind, mode, 4 + i)

    def gather_wait(kind, mode):
        for i in range(2, 6):
            gather_recv(kind, mode, i)

    staged = (dd, du)
    got = (rd, ru)
    own_deliver = {}

    def positions():
        for mode in range(2):
            for q in range(8):
                g = device(mode, q)

                def one(j, carry, mode=mode, q=q, g=g):
                    s = stor[mids[g, j]]
                    if mode == 1:
                        s = ((s // 16) % 4) * 64 + (s // 64) * 16 + s % 16
                    pos[mode * 8 + q, j] = s
                    return carry

                lax.fori_loop(0, MISS, one, 0, unroll=14)

    def select(kind, mode, t, o):
        def one(j, carry):
            at = pos[mode * 8 + t, j]
            staged[kind][mode, o, j] = stock[kind][mode, at]
            return carry

        lax.fori_loop(0, MISS, one, 0, unroll=4)

    def deliver(kind, offsets):
        for o in offsets:
            for mode in range(2):
                q = member[mode]
                t = partner(mode, o)
                select(kind, mode, t, o)
                if o:
                    cp = remote(
                        staged[kind].at[mode, o], got[kind].at[mode, q],
                        d_s.at[mode, kind, o - 1], d_r.at[mode, kind, o - 1], device(mode, t), z,
                    )
                    cp.start()
                    sends.append(cp)
                else:
                    cp = pltpu.make_async_copy(
                        staged[kind].at[mode, o], got[kind].at[mode, q], loc_sem.at[mode, 2 + kind]
                    )
                    cp.start()
                    own_deliver[mode, kind] = cp

    def deliver_wait(kind, offsets):
        for o in offsets:
            for mode in range(2):
                if o == 0:
                    own_deliver[mode, kind].wait()
                    continue
                f = partner(mode, o, True)
                remote(
                    staged[kind].at[mode, o], got[kind].at[mode, f],
                    d_s.at[mode, kind, o - 1], d_r.at[mode, kind, o - 1], device(mode, f), z,
                ).wait_recv()

    def ring_copy(way, k, i):
        to = (z + 1) % NZ if way == 0 else (z + NZ - 1) % NZ
        rows = pl.ds(pl.multiple_of(i * 256, 256), 256)
        return remote(
            zs.at[way, k, rows], zr.at[way, k, rows], z_s.at[way, k, i], z_r.at[way, k, i], p, to
        )

    def ring_step(k, first=0, last=3):
        dist = 4 - (k + 1) // 2

        def tile(i, carry):
            rows = pl.ds(pl.multiple_of(i * 256, 256), 256)
            for way in range(2):
                d = dist if way == 0 else NZ - dist
                half = (k + way) % 2
                if k >= 2:
                    ring_copy(way, k - 2, i).wait_recv()
                v = jnp.dot(
                    att[rows, :], w[d, :, HALF * half:HALF * half + HALF],
                    preferred_element_type=F32,
                )
                if k >= 2:
                    v = v + zr[way, k - 2, rows, :].astype(F32)
                zs[way, k, rows, :] = v.astype(BF)
                ring_copy(way, k, i).start()
            return carry

        lax.fori_loop(first, last, tile, 0)

    def ring_drain():
        for k in range(7):
            for way in range(2):
                for i in range(3):
                    ring_copy(way, k, i).wait_send()

    def own_chunk():
        loads[0].wait()

        def tile(i, carry):
            rows = pl.ds(pl.multiple_of(i * 256, 256), 256)
            for half in range(2):
                cols = slice(HALF * half, HALF * half + HALF)
                base[rows, cols] = jnp.dot(
                    att[rows, :], w[0, :, cols], preferred_element_type=F32
                )
            return carry

        lax.fori_loop(0, 3, tile, 0)

    def row_positions():
        def one(s, carry):
            start, missed, hit = carry
            is_miss = jnp.logical_and(missed < MISS, mslots[0, jnp.minimum(missed, MISS - 1)] == s)
            slot_s[0, s] = start
            slot_s[1, s] = jnp.where(is_miss, HITS + missed, hit)
            step = jnp.where(is_miss, 1, 0)
            return start + seg[0, s], missed + step, hit + 1 - step

        lax.fori_loop(0, USED, one, (jnp.int32(0), jnp.int32(0), jnp.int32(0)))

        def tile(i, carry):
            rows = i * 96 + lax.broadcasted_iota(jnp.int32, (96, 128), 0)

            def slot(s, v):
                return jnp.where(rows >= slot_s[0, s], slot_s[1, s], v)

            prow[pl.ds(pl.multiple_of(i * 96, 96), 96), :] = lax.fori_loop(
                0, USED, slot, jnp.zeros((96, 128), jnp.int32), unroll=8
            )
            return carry

        lax.fori_loop(0, 8, tile, 0)

    def shrink_hits():
        lane = lax.broadcasted_iota(jnp.int32, (384, 128), 1)
        for t in range(2):
            rows = slice(384 * t, 384 * t + 384)
            pm = prow[rows, :] - lane // 32
            for mode in range(2):
                hit = cd[:, 32 * mode:32 * mode + 32, :].reshape(HITS * 32, KD)
                xh = lax.dot_general(att[rows, :], hit, NT, preferred_element_type=F32)
                acc = jnp.where(pm == 0, xh[:, 0:128], 0.0)
                for b in range(1, 3):
                    acc = acc + jnp.where(pm == 4 * b, xh[:, 128 * b:128 * b + 128], 0.0)
                hacc[mode, rows, :] = acc

    def shrink(i):
        lane = lax.broadcasted_iota(jnp.int32, (256, 128), 1)
        rows = slice(256 * i, 256 * i + 256)
        pm = prow[rows, :] - lane // 32
        sums = []
        for mode in range(2):
            acc = hacc[mode, rows, :]
            miss = jnp.concatenate(
                [rd[mode, q].reshape(MISS * 32, 128) for q in range(8)], axis=1
            )
            xm = lax.dot_general(att[rows, :], miss, NT, preferred_element_type=F32)
            for b in range(7):
                acc = acc + jnp.where(pm == HITS + 4 * b, xm[:, 128 * b:128 * b + 128], 0.0)
            acc = acc + pltpu.roll(acc, 64, 1)
            acc = acc + pltpu.roll(acc, 32, 1)
            sums.append(acc)
        full = jnp.where((lane // 32) % 2 == 0, sums[0], sums[1])
        part[i] = jnp.where(lane[0:128] < 64, full[0:128], full[128:256])
        for o in (4, 3, 5, 2, 6, 1, 7):
            cp = scatter_copy(i, o)
            cp.start()
            sends.append(cp)

    def scatter_copy(i, o):
        t = (z + o) % NZ
        return remote(
            part.at[i, pl.ds(pl.multiple_of(t * 16, 16), 16)], ar.at[i, o - 1],
            a_s.at[0, i, o - 1], a_r.at[0, i, o - 1], p, t,
        )

    def ranks_copy(i, o, src):
        t = (z + o) % NZ
        dst = sh.at[i, pl.ds(pl.multiple_of(src * 16, 16), 16)]
        return remote(own_sh.at[i], dst, a_s.at[1, i, o - 1], a_r.at[1, i, o - 1], p, t)

    def own_ranks_copy(i):
        return pltpu.make_async_copy(
            own_sh.at[i], sh.at[i, pl.ds(pl.multiple_of(z * 16, 16), 16)], in_sem.at[14 + i]
        )

    def rank_sums(i):
        total = part[i, pl.ds(pl.multiple_of(z * 16, 16), 16), :]
        for o in range(1, NZ):
            scatter_copy(i, o).wait_recv()
        for o in range(7):
            total = total + ar[i, o]
        own_sh[i] = total.astype(BF)
        own_ranks_copy(i).start()
        for o in (4, 3, 5, 2, 6, 1, 7):
            cp = ranks_copy(i, o, z)
            cp.start()
            sends.append(cp)

    def expand(i):
        own_ranks_copy(i).wait()
        for o in range(1, NZ):
            ranks_copy(i, o, (z + NZ - o) % NZ).wait_recv()
        lane = lax.broadcasted_iota(jnp.int32, (128, 128), 1)
        row_e = lax.broadcasted_iota(jnp.int32, (128, 512), 0)
        col_e = lax.broadcasted_iota(jnp.int32, (128, 512), 1)
        s = sh[i]
        for t in range(2):
            rows = slice(256 * i + 128 * t, 256 * i + 128 * t + 128)
            pick = row_e == 64 * t + (col_e // 128) * 16 + col_e % 16
            spread = jnp.dot(s, jnp.where(pick, 1.0, 0.0).astype(BF), preferred_element_type=F32)
            pm = prow[rows, :] - lane // 16
            for b in range(5):
                m = pm == 8 * b
                for rb in range(4):
                    sexp[rows, 640 * rb + 128 * b:640 * rb + 128 * b + 128] = jnp.where(
                        m, spread[:, 128 * rb:128 * rb + 128], 0.0
                    ).astype(BF)

    def grow(i):
        rows = slice(256 * i, 256 * i + 256)
        acc = base[rows, :]
        for rb in range(4):
            mode, first = rb // 2, (rb % 2) * 4
            up = jnp.concatenate(
                [
                    cu[:, 16 * rb:16 * rb + 16, :].reshape(HITS * 16, CHUNK),
                    jnp.concatenate(
                        [ru[mode, first + cb].reshape(MISS * 16, 128) for cb in range(4)], axis=1
                    ),
                ],
                axis=0,
            )
            acc = acc + jnp.dot(
                sexp[rows, 640 * rb:640 * rb + 640], up, preferred_element_type=F32
            )
        base[rows, :] = acc

    def finish(i):
        for way in range(2):
            for k in (5, 6):
                ring_copy(way, k, i).wait_recv()
        rows = slice(256 * i, 256 * i + 256)
        for half in range(2):
            cols = slice(HALF * half, HALF * half + HALF)
            k0 = 6 if half == 0 else 5
            out_ref[rows, cols] = (
                base[rows, cols]
                + zr[0, k0, rows, :].astype(F32)
                + zr[1, 11 - k0, rows, :].astype(F32)
            ).astype(BF)

    loads["pd"].wait()
    spread_start(0)
    loads["att"].wait()
    loads[4].wait()
    ring_step(0)
    loads["pu"].wait()
    spread_start(1)
    loads[3].wait()
    loads[5].wait()
    ring_step(1)
    for mode in range(2):
        spread_wait(0, mode)
        gather_start(0, mode)
    for k in range(4):
        loads["int", k].wait()
    positions()
    ring_step(2)
    for mode in range(2):
        gather_forward(0, mode)
    row_positions()
    for mode in range(2):
        spread_wait(1, mode)
    loads[2].wait()
    loads[6].wait()
    ring_step(3)
    for mode in range(2):
        gather_start(1, mode)
    for mode in range(2):
        gather_wait(0, mode)
    deliver(0, (4, 5, 2, 6, 3, 7, 1, 0))
    for mode in range(2):
        gather_forward(1, mode)
    ring_step(4)
    loads["cd"].wait()
    shrink_hits()
    own_chunk()
    loads[1].wait()
    loads[7].wait()
    ring_step(5)
    loads["cu"].wait()
    ring_step(6, 0, 2)
    for mode in range(2):
        gather_wait(1, mode)
    deliver_wait(0, (0, 1, 4, 5, 2))
    deliver(1, (4, 5, 2, 6, 3, 7, 1, 0))
    deliver_wait(0, (6, 3, 7))
    for i in range(3):
        shrink(i)
    for i in range(3):
        rank_sums(i)
    ring_step(6, 2, 3)
    expand(0)
    deliver_wait(1, range(8))
    grow(0)
    expand(1)
    grow(1)
    expand(2)
    grow(2)
    for i in range(3):
        finish(i)
    ring_drain()
    for cp in sends:
        cp.wait_send()


def per_device(*args):
    hbm = pl.BlockSpec(memory_space=pl.ANY)
    dma = pltpu.SemaphoreType.DMA
    return pl.pallas_call(
        kernel,
        out_shape=jax.ShapeDtypeStruct((ROWS, CHUNK), BF),
        in_specs=[hbm] * 10,
        out_specs=pl.BlockSpec(memory_space=pltpu.VMEM),
        scratch_shapes=[
            pltpu.VMEM((ROWS, KD), BF),
            pltpu.VMEM((NZ, KD, CHUNK), BF),
            pltpu.VMEM((HITS, 64, KD), BF),
            pltpu.VMEM((HITS, 64, CHUNK), BF),
            pltpu.VMEM((8, 64, KD), BF),
            pltpu.VMEM((8, 64, CHUNK), BF),
            pltpu.VMEM((2, 256, 32, 128), BF),
            pltpu.VMEM((2, 256, 16, 128), BF),
            pltpu.VMEM((2, 8, MISS, 32, 128), BF),
            pltpu.VMEM((2, 8, MISS, 16, 128), BF),
            pltpu.VMEM((2, 8, MISS, 32, 128), BF),
            pltpu.VMEM((2, 8, MISS, 16, 128), BF),
            pltpu.VMEM((2, 7, ROWS, HALF), BF),
            pltpu.VMEM((2, 7, ROWS, HALF), BF),
            pltpu.VMEM((ROWS, CHUNK), F32),
            pltpu.VMEM((ROWS, 128), jnp.int32),
            pltpu.VMEM((2, ROWS, 128), F32),
            pltpu.VMEM((3, 128, 128), F32),
            pltpu.VMEM((3, 7, 16, 128), F32),
            pltpu.VMEM((3, 16, 128), BF),
            pltpu.VMEM((3, 128, 128), BF),
            pltpu.VMEM((ROWS, 2560), BF),
            pltpu.SMEM((1, USED), jnp.int32),
            pltpu.SMEM((1, MISS), jnp.int32),
            pltpu.SMEM((32, MISS), jnp.int32),
            pltpu.SMEM((256,), jnp.int32),
            pltpu.SMEM((16, MISS), jnp.int32),
            pltpu.SMEM((2, USED), jnp.int32),
            dma((21,)),
            dma((2, 4)),
            dma((2, 2, 7)),
            dma((2, 2, 7)),
            dma((2, 2, 6)),
            dma((2, 2, 6)),
            dma((2, 2, 7)),
            dma((2, 2, 7)),
            dma((2, 7, 3)),
            dma((2, 7, 3)),
            dma((2, 3, 7)),
            dma((2, 3, 7)),
        ],
        compiler_params=pltpu.CompilerParams(
            collective_id=0, has_side_effects=True, vmem_limit_bytes=60 * 1024 * 1024
        ),
        cost_estimate=pl.CostEstimate(
            flops=12_500_000_000, bytes_accessed=14_000_000, transcendentals=0
        ),
        name="lora_projection",
    )(*args)


def solution(mesh):
    return jax.shard_map(
        per_device,
        mesh=mesh,
        in_specs=(
            P("pool", "tp"),
            P("tp", None),
            P("pool", None, "tp"),
            P("pool", None, "tp"),
            P("pool", None, "tp"),
            P("pool", None, "tp"),
            P("pool", None),
            P("pool", None),
            P(),
            P(),
        ),
        out_specs=P("pool", "tp"),
        check_vma=False,
    )
```

time: 94.7 us -> 89.6 us (0.946)
  Pallas kernels: 91.9 us -> 87.4 us
    pallas_call x1, Pallas kernels: 91.9 us -> 87.4 us  [per_device(): pl.pallas_call(kernel, out_shape=jax.ShapeDtypeStruct((ROWS, CHUNK), BF),...]
where the time goes in v2:
time: 89.6 us; the launch traced here: 89.5 us
  Pallas kernels  87.4 us (98%)
  local copies, waits for them, and re-layouts  2.06 us (2%)
    pallas_call x1, Pallas kernels, per_device(): pl.pallas_call(kernel, out_shape=jax.ShapeDtypeStruct((ROWS, CHUNK), BF),...  87.4 us
    unnamed x1, local copies, waits for them, and re-layouts  2.06 us

profile of v2, /device:TPU:1, one launch (start us, length us, event | category | flops | bytes accessed | tf_op | source)
XLA Modules:
  0.0 89.5 jit_solution(2588580617494948612)
XLA Ops:
  0.0 87.4 %lora_projection.1 = bf16[768,512]{1,0:T(8,128)(2,1)} custom-call(bf16[768,1024]{1,0:T(8,128)(2,1)} %att_h.1, bf16[1024,4096]{1,0:T(8,128)(2,1)} %w_h.1, bf16[12,64,1024]{2,1,0:T(8,128)(2,1)} %cd_h.1, bf16[12,64,512]{2,1,0:T(8,128)(2,1)} %cu_h.1, bf16[8,64,1024]{2,1,0:T(8,128)(2,1)} %pd_h.1, bf16[8,64,512]{2,1,0:T(8,128)(2,1)} %pu_h.1, s32[1,40]{1,0:T(1,128)} %seg_h.1, ...), custom_call_target="tpu_custom_call" | custom-call | flops 12499999744 | bytes 14000000 | tf_op jit(solution)/shard_map/lora_projection/pallas_call | solution.py:488
  87.4 2.1 %copy.12 = bf16[768,512]{1,0:T(8,128)(2,1)} copy(bf16[768,512]{1,0:T(8,128)(2,1)} %lora_projection.1) | data formatting | bytes 1572864

commit v3 on v2

--- a/solution.py
+++ b/solution.py
@@ -26,7 +26,7 @@
     out_ref,
     att, w, cd, cu, pd, pu, sd, su, dd, du, rd, ru, zr, zs, base, prow, hacc, part, ar, own_sh, sh, sexp,
     seg, mslots, mids, stor, pos, slot_s,
-    in_sem, loc_sem, p1_s, p1_r, g_s, g_r, d_s, d_r, z_s, z_r, a_s, a_r,
+    out_v, in_sem, loc_sem, p1_s, p1_r, g_s, g_r, d_s, d_r, z_s, z_r, a_s, a_r,
 ):
     p = lax.axis_index("pool")
     z = lax.axis_index("tp")
@@ -53,37 +53,43 @@
         return place * 2 + (c + e) % 2
 
     near_last = (4, 5, 2, 6, 3, 7, 1)
-    sends = []
+    def await_recv(ref, sem):
+        remote(ref, ref, z_s.at[0], sem, p, (z + 1) % NZ).wait_recv()
+
+    def await_send(ref, sem):
+        remote(ref, ref, sem, z_r.at[0], p, (z + 1) % NZ).wait_send()
+
 
     bar = pltpu.get_barrier_semaphore()
-    for mode in range(2):
-        for o in range(1, 8):
+    for o in (4, 3, 5, 2, 6, 1, 7):
+        pl.semaphore_signal(bar, inc=1, device_id=(p, (z + o) % NZ), device_id_type=MESH)
+    for o in near_last:
+        for mode in range(2):
             pl.semaphore_signal(
                 bar, inc=1, device_id=(device(mode, partner(mode, o)), z), device_id_type=MESH
             )
-    for o in range(1, NZ):
-        pl.semaphore_signal(bar, inc=1, device_id=(p, (z + o) % NZ), device_id_type=MESH)
 
     loads = {}
-    loads["att"] = pltpu.make_async_copy(att_h, att, in_sem.at[8])
-    loads["cd"] = pltpu.make_async_copy(cd_h, cd, in_sem.at[9])
-    loads["cu"] = pltpu.make_async_copy(cu_h, cu, in_sem.at[10])
-    loads["pd"] = pltpu.make_async_copy(pd_h, pd, in_sem.at[12])
-    loads["pu"] = pltpu.make_async_copy(pu_h, pu, in_sem.at[13])
     for k, (src, dst) in enumerate(
-        ((seg_h, seg), (mslots_h, mslots), (mids_h, mids), (stor_h, stor))
+        (
+            (pd_h, pd), (pu_h, pu), (att_h, att), (cd_h, cd), (cu_h, cu),
+            (seg_h, seg), (mslots_h, mslots), (mids_h, mids), (stor_h, stor),
+        )
     ):
-        loads["int", k] = pltpu.make_async_copy(src, dst, in_sem.at[17 + k])
-    for k in range(NZ):
+        loads[k] = pltpu.make_async_copy(src, dst, in_sem.at[k])
+
+    def weight_copy(k):
         d = (z + k) % NZ
-        loads[k] = pltpu.make_async_copy(
-            w_h.at[:, pl.ds(pl.multiple_of(d * CHUNK, CHUNK), CHUNK)], w.at[k], in_sem.at[k]
-        )
-    for k in ("pd", "pu", "att", 4, 3, 5):
+        return pltpu.make_async_copy(
+            w_h.at[:, pl.ds(pl.multiple_of(d * CHUNK, CHUNK), CHUNK)],
+            w.at[k], in_sem.at[9 if k == 4 else 10],
+        )
+
+    for k in range(3):
         loads[k].start()
-    for k in range(4):
-        loads["int", k].start()
-    for k in (2, 6, 1, 7, 0, "cd", "cu"):
+    for k in (4, 3, 5, 2, 6, 1, 7, 0):
+        weight_copy(k).start()
+    for k in (5, 6, 7, 8, 3, 4):
         loads[k].start()
     pl.semaphore_wait(bar, 21)
 
@@ -101,36 +107,25 @@
     def spread_dst(kind, mode, q):
         return stock[kind].at[mode, pl.ds(ring[mode] * 64 + q * 8, 8)]
 
-    own_spread = {}
-
     def spread_start(kind):
         for o in near_last:
             for mode in range(2):
                 q = member[mode]
                 t = partner(mode, o)
-                cp = remote(
+                remote(
                     spread_src(kind, mode, t), spread_dst(kind, mode, q),
-                    p1_s.at[mode, kind, o - 1], p1_r.at[mode, kind, o - 1], device(mode, t), z,
-                )
-                cp.start()
-                sends.append(cp)
+                    p1_s.at[kind], p1_r.at[kind], device(mode, t), z,
+                ).start()
         for mode in range(2):
             q = member[mode]
-            cp = pltpu.make_async_copy(
-                spread_src(kind, mode, q), spread_dst(kind, mode, q), loc_sem.at[mode, kind]
-            )
-            cp.start()
-            own_spread[mode, kind] = cp
-
-    def spread_wait(kind, mode):
-        q = member[mode]
-        own_spread[mode, kind].wait()
-        for o in range(1, 8):
-            f = partner(mode, o, True)
-            remote(
-                spread_dst(kind, mode, f), spread_dst(kind, mode, f),
-                p1_s.at[mode, kind, o - 1], p1_r.at[mode, kind, o - 1], device(mode, f), z,
-            ).wait_recv()
+            pltpu.make_async_copy(
+                spread_src(kind, mode, q), spread_dst(kind, mode, q), loc_sem.at[0, kind]
+            ).start()
+
+    def spread_wait(kind):
+        both = stock[kind].at[0, pl.ds(0, 16)]
+        pltpu.make_async_copy(both, both, loc_sem.at[0, kind]).wait()
+        await_recv(stock[kind].at[0, pl.ds(0, 112)], p1_r.at[kind])
 
     def shard(kind, mode, r, first, count):
         return stock[kind].at[mode, pl.ds(((ring[mode] + r) % 4) * 64 + first, count)]
@@ -138,38 +133,30 @@
     def gather_copy(kind, mode, i, ref):
         step = 1 if i % 2 == 0 else 3
         return remote(
-            ref, ref, g_s.at[mode, kind, i], g_r.at[mode, kind, i], ring_next(mode, step), z
+            ref, ref, g_s.at[kind], g_r.at[kind, 0 if i < 2 else 1], ring_next(mode, step), z
         )
 
     halves = ((0, 0), (0, 32), (0, 32), (0, 0), (3, 0), (1, 32))
 
-    def gather_send(kind, mode, i):
+    def gather_send(kind, i):
         r, first = halves[i]
-        cp = gather_copy(kind, mode, i, shard(kind, mode, r, first, 32))
-        cp.start()
-        sends.append(cp)
-
-    def gather_recv(kind, mode, i):
-        r, first = halves[i]
-        r = (r + (3 if i % 2 == 0 else 1)) % 4
-        gather_copy(kind, mode, i, shard(kind, mode, r, first, 32)).wait_recv()
-
-    def gather_start(kind, mode):
+        for mode in range(2):
+            gather_copy(kind, mode, i, shard(kind, mode, r, first, 32)).start()
+
+    def gather_start(kind):
         for i in range(4):
-            gather_send(kind, mode, i)
-
-    def gather_forward(kind, mode):
-        for i in range(2):
-            gather_recv(kind, mode, i)
-            gather_send(kind, mode, 4 + i)
-
-    def gather_wait(kind, mode):
-        for i in range(2, 6):
-            gather_recv(kind, mode, i)
+            gather_send(kind, i)
+
+    def gather_forward(kind):
+        await_recv(stock[kind].at[0, pl.ds(0, 128)], g_r.at[kind, 0])
+        for i in range(4, 6):
+            gather_send(kind, i)
+
+    def gather_wait(kind):
+        await_recv(stock[kind].at[0], g_r.at[kind, 1])
 
     staged = (dd, du)
     got = (rd, ru)
-    own_deliver = {}
 
     def positions():
         for mode in range(2):
@@ -191,57 +178,42 @@
             staged[kind][mode, o, j] = stock[kind][mode, at]
             return carry
 
-        lax.fori_loop(0, MISS, one, 0, unroll=4)
-
-    def deliver(kind, offsets):
-        for o in offsets:
+        lax.fori_loop(0, MISS, one, 0, unroll=14)
+
+    def deliver(kind):
+        for o in near_last + (0,):
             for mode in range(2):
                 q = member[mode]
                 t = partner(mode, o)
                 select(kind, mode, t, o)
+                src, dst = staged[kind].at[mode, o], got[kind].at[mode, q]
                 if o:
-                    cp = remote(
-                        staged[kind].at[mode, o], got[kind].at[mode, q],
-                        d_s.at[mode, kind, o - 1], d_r.at[mode, kind, o - 1], device(mode, t), z,
-                    )
-                    cp.start()
-                    sends.append(cp)
+                    remote(src, dst, d_s.at[kind], d_r.at[kind], device(mode, t), z).start()
                 else:
-                    cp = pltpu.make_async_copy(
-                        staged[kind].at[mode, o], got[kind].at[mode, q], loc_sem.at[mode, 2 + kind]
-                    )
-                    cp.start()
-                    own_deliver[mode, kind] = cp
-
-    def deliver_wait(kind, offsets):
-        for o in offsets:
-            for mode in range(2):
-                if o == 0:
-                    own_deliver[mode, kind].wait()
-                    continue
-                f = partner(mode, o, True)
-                remote(
-                    staged[kind].at[mode, o], got[kind].at[mode, f],
-                    d_s.at[mode, kind, o - 1], d_r.at[mode, kind, o - 1], device(mode, f), z,
-                ).wait_recv()
+                    pltpu.make_async_copy(src, dst, loc_sem.at[1, kind]).start()
+
+    def deliver_wait(kind):
+        both = staged[kind].at[0, pl.ds(0, 2)]
+        pltpu.make_async_copy(both, both, loc_sem.at[1, kind]).wait()
+        await_recv(staged[kind].at[:, pl.ds(1, 7)], d_r.at[kind])
 
     def ring_copy(way, k, i):
         to = (z + 1) % NZ if way == 0 else (z + NZ - 1) % NZ
         rows = pl.ds(pl.multiple_of(i * 256, 256), 256)
         return remote(
-            zs.at[way, k, rows], zr.at[way, k, rows], z_s.at[way, k, i], z_r.at[way, k, i], p, to
+            zs.at[way, k, rows], zr.at[way, k, rows], z_s.at[0], z_r.at[k], p, to
         )
 
     def ring_step(k, first=0, last=3):
         dist = 4 - (k + 1) // 2
+        if k >= 2 and first == 0:
+            await_recv(zr.at[:, k - 2], z_r.at[k - 2])
 
         def tile(i, carry):
             rows = pl.ds(pl.multiple_of(i * 256, 256), 256)
             for way in range(2):
                 d = dist if way == 0 else NZ - dist
                 half = (k + way) % 2
-                if k >= 2:
-                    ring_copy(way, k - 2, i).wait_recv()
                 v = jnp.dot(
                     att[rows, :], w[d, :, HALF * half:HALF * half + HALF],
                     preferred_element_type=F32,
@@ -254,14 +226,7 @@
 
         lax.fori_loop(first, last, tile, 0)
 
-    def ring_drain():
-        for k in range(7):
-            for way in range(2):
-                for i in range(3):
-                    ring_copy(way, k, i).wait_send()
-
     def own_chunk():
-        loads[0].wait()
 
         def tile(i, carry):
             rows = pl.ds(pl.multiple_of(i * 256, 256), 256)
@@ -330,44 +295,38 @@
         full = jnp.where((lane // 32) % 2 == 0, sums[0], sums[1])
         part[i] = jnp.where(lane[0:128] < 64, full[0:128], full[128:256])
         for o in (4, 3, 5, 2, 6, 1, 7):
-            cp = scatter_copy(i, o)
-            cp.start()
-            sends.append(cp)
+            scatter_copy(i, o).start()
 
     def scatter_copy(i, o):
         t = (z + o) % NZ
         return remote(
             part.at[i, pl.ds(pl.multiple_of(t * 16, 16), 16)], ar.at[i, o - 1],
-            a_s.at[0, i, o - 1], a_r.at[0, i, o - 1], p, t,
+            a_s.at[0], a_r.at[0, i], p, t,
         )
 
     def ranks_copy(i, o, src):
         t = (z + o) % NZ
         dst = sh.at[i, pl.ds(pl.multiple_of(src * 16, 16), 16)]
-        return remote(own_sh.at[i], dst, a_s.at[1, i, o - 1], a_r.at[1, i, o - 1], p, t)
+        return remote(own_sh.at[i], dst, a_s.at[1], a_r.at[1, i], p, t)
 
     def own_ranks_copy(i):
         return pltpu.make_async_copy(
-            own_sh.at[i], sh.at[i, pl.ds(pl.multiple_of(z * 16, 16), 16)], in_sem.at[14 + i]
+            own_sh.at[i], sh.at[i, pl.ds(pl.multiple_of(z * 16, 16), 16)], in_sem.at[11 + i]
         )
 
     def rank_sums(i):
         total = part[i, pl.ds(pl.multiple_of(z * 16, 16), 16), :]
-        for o in range(1, NZ):
-            scatter_copy(i, o).wait_recv()
+        await_recv(ar.at[i], a_r.at[0, i])
         for o in range(7):
             total = total + ar[i, o]
         own_sh[i] = total.astype(BF)
         own_ranks_copy(i).start()
         for o in (4, 3, 5, 2, 6, 1, 7):
-            cp = ranks_copy(i, o, z)
-            cp.start()
-            sends.append(cp)
+            ranks_copy(i, o, z).start()
 
     def expand(i):
         own_ranks_copy(i).wait()
-        for o in range(1, NZ):
-            ranks_copy(i, o, (z + NZ - o) % NZ).wait_recv()
+        await_recv(su.at[0, pl.ds(0, 7)], a_r.at[1, i])
         lane = lax.broadcasted_iota(jnp.int32, (128, 128), 1)
         row_e = lax.broadcasted_iota(jnp.int32, (128, 512), 0)
         col_e = lax.broadcasted_iota(jnp.int32, (128, 512), 1)
@@ -403,83 +362,85 @@
             )
         base[rows, :] = acc
 
+    def out_copy(i):
+        rows = pl.ds(256 * i, 256)
+        return pltpu.make_async_copy(out_v.at[rows], out_ref.at[rows], in_sem.at[14 + i])
+
     def finish(i):
-        for way in range(2):
-            for k in (5, 6):
-                ring_copy(way, k, i).wait_recv()
         rows = slice(256 * i, 256 * i + 256)
         for half in range(2):
             cols = slice(HALF * half, HALF * half + HALF)
             k0 = 6 if half == 0 else 5
-            out_ref[rows, cols] = (
+            out_v[rows, cols] = (
                 base[rows, cols]
                 + zr[0, k0, rows, :].astype(F32)
                 + zr[1, 11 - k0, rows, :].astype(F32)
             ).astype(BF)
-
-    loads["pd"].wait()
+        out_copy(i).start()
+
+    def drain():
+        for kind in range(2):
+            await_send(stock[kind].at[0, pl.ds(0, 112)], p1_s.at[kind])
+            await_send(stock[kind].at[:, pl.ds(0, 192)], g_s.at[kind])
+            await_send(staged[kind].at[:, pl.ds(1, 7)], d_s.at[kind])
+        await_send(zs, z_s.at[0])
+        await_send(ar, a_s.at[0])
+        await_send(su.at[0, pl.ds(0, 21)], a_s.at[1])
+        for i in range(3):
+            out_copy(i).wait()
+
+    loads[0].wait()
     spread_start(0)
-    loads["att"].wait()
-    loads[4].wait()
+    loads[2].wait()
+    weight_copy(4).wait()
     ring_step(0)
-    loads["pu"].wait()
+    loads[1].wait()
     spread_start(1)
-    loads[3].wait()
-    loads[5].wait()
+    pltpu.make_async_copy(w.at[pl.ds(0, 7)], w.at[pl.ds(0, 7)], in_sem.at[10]).wait()
     ring_step(1)
-    for mode in range(2):
-        spread_wait(0, mode)
-        gather_start(0, mode)
-    for k in range(4):
-        loads["int", k].wait()
+    spread_wait(0)
+    gather_start(0)
+    for k in range(5, 9):
+        loads[k].wait()
     positions()
     ring_step(2)
-    for mode in range(2):
-        gather_forward(0, mode)
+    gather_forward(0)
     row_positions()
-    for mode in range(2):
-        spread_wait(1, mode)
-    loads[2].wait()
-    loads[6].wait()
+    spread_wait(1)
     ring_step(3)
-    for mode in range(2):
-        gather_start(1, mode)
-    for mode in range(2):
-        gather_wait(0, mode)
-    deliver(0, (4, 5, 2, 6, 3, 7, 1, 0))
-    for mode in range(2):
-        gather_forward(1, mode)
-    ring_step(4)
-    loads["cd"].wait()
+    gather_start(1)
+    loads[3].wait()
+    loads[4].wait()
     shrink_hits()
     own_chunk()
-    loads[1].wait()
-    loads[7].wait()
+    gather_wait(0)
+    deliver(0)
+    gather_forward(1)
+    ring_step(4)
     ring_step(5)
-    loads["cu"].wait()
     ring_step(6, 0, 2)
-    for mode in range(2):
-        gather_wait(1, mode)
-    deliver_wait(0, (0, 1, 4, 5, 2))
-    deliver(1, (4, 5, 2, 6, 3, 7, 1, 0))
-    deliver_wait(0, (6, 3, 7))
-    for i in range(3):
-        shrink(i)
-    for i in range(3):
-        rank_sums(i)
+    deliver_wait(0)
+    shrink(0)
+    gather_wait(1)
+    deliver(1)
+    shrink(1)
+    shrink(2)
+    rank_sums(0)
+    rank_sums(1)
     ring_step(6, 2, 3)
+    rank_sums(2)
     expand(0)
-    deliver_wait(1, range(8))
+    deliver_wait(1)
     grow(0)
     expand(1)
     grow(1)
     expand(2)
     grow(2)
+    await_recv(zr.at[:, 5], z_r.at[5])
+    await_recv(zr.at[:, 6], z_r.at[6])
     for i in range(3):
         finish(i)
-    ring_drain()
-    for cp in sends:
-        cp.wait_send()
+    drain()
 
 
 def per_device(*args):
@@ -489,7 +450,7 @@
         kernel,
         out_shape=jax.ShapeDtypeStruct((ROWS, CHUNK), BF),
         in_specs=[hbm] * 10,
-        out_specs=pl.BlockSpec(memory_space=pltpu.VMEM),
+        out_specs=hbm,
         scratch_shapes=[
             pltpu.VMEM((ROWS, KD), BF),
             pltpu.VMEM((NZ, KD, CHUNK), BF),
@@ -519,18 +480,19 @@
             pltpu.SMEM((256,), jnp.int32),
             pltpu.SMEM((16, MISS), jnp.int32),
             pltpu.SMEM((2, USED), jnp.int32),
-            dma((21,)),
-            dma((2, 4)),
-            dma((2, 2, 7)),
-            dma((2, 2, 7)),
-            dma((2, 2, 6)),
-            dma((2, 2, 6)),
-            dma((2, 2, 7)),
-            dma((2, 2, 7)),
-            dma((2, 7, 3)),
-            dma((2, 7, 3)),
-            dma((2, 3, 7)),
-            dma((2, 3, 7)),
+            pltpu.VMEM((ROWS, CHUNK), BF),
+            dma((17,)),
+            dma((2, 2)),
+            dma((2,)),
+            dma((2,)),
+            dma((2,)),
+            dma((2, 2)),
+            dma((2,)),
+            dma((2,)),
+            dma((1,)),
+            dma((7,)),
+            dma((2,)),
+            dma((2, 3)),
         ],
         compiler_params=pltpu.CompilerParams(
             collective_id=0, has_side_effects=True, vmem_limit_bytes=60 * 1024 * 1024

time: 89.6 us -> 86 us (0.960)
  Pallas kernels: 87.4 us -> 83.8 us
    pallas_call x1, Pallas kernels: 87.4 us -> 83.8 us  [per_device(): pl.pallas_call(kernel, out_shape=jax.ShapeDtypeStruct((ROWS, CHUNK), BF),...]
where the time goes in v3:
time: 86 us; the launch traced here: 85.9 us
  Pallas kernels  83.8 us (97%)
  local copies, waits for them, and re-layouts  2.06 us (2%)
    pallas_call x1, Pallas kernels, per_device(): pl.pallas_call(kernel, out_shape=jax.ShapeDtypeStruct((ROWS, CHUNK), BF),...  83.8 us
    unnamed x1, local copies, waits for them, and re-layouts  2.06 us

profile of v3, /device:TPU:1, one launch (start us, length us, event | category | flops | bytes accessed | tf_op | source)
XLA Modules:
  0.0 85.9 jit_solution(17025183473110350893)
XLA Ops:
  0.0 83.8 %lora_projection.1 = bf16[768,512]{1,0:T(8,128)(2,1)} custom-call(bf16[768,1024]{1,0:T(8,128)(2,1)} %att_h.1, bf16[1024,4096]{1,0:T(8,128)(2,1)} %w_h.1, bf16[12,64,1024]{2,1,0:T(8,128)(2,1)} %cd_h.1, bf16[12,64,512]{2,1,0:T(8,128)(2,1)} %cu_h.1, bf16[8,64,1024]{2,1,0:T(8,128)(2,1)} %pd_h.1, bf16[8,64,512]{2,1,0:T(8,128)(2,1)} %pu_h.1, s32[1,40]{1,0:T(1,128)} %seg_h.1, ...), custom_call_target="tpu_custom_call" | custom-call | flops 12499999744 | bytes 14000000 | tf_op jit(solution)/shard_map/lora_projection/pallas_call | solution.py:449
  83.8 2.1 %copy.12 = bf16[768,512]{1,0:T(8,128)(2,1)} copy(bf16[768,512]{1,0:T(8,128)(2,1)} %lora_projection.1) | data formatting | bytes 1572864

commit v4 on v3

--- a/solution.py
+++ b/solution.py
@@ -10,6 +10,7 @@
 USED = 40
 MISS = 28
 HITS = 12
+FIRST_MISS = 16
 ROWS = 768
 KD = 1024
 CHUNK = 512
@@ -24,7 +25,7 @@
 def kernel(
     att_h, w_h, cd_h, cu_h, pd_h, pu_h, seg_h, mslots_h, mids_h, stor_h,
     out_ref,
-    att, w, cd, cu, pd, pu, sd, su, dd, du, rd, ru, zr, zs, base, prow, hacc, part, ar, own_sh, sh, sexp,
+    att, w, cd, cu, pd, pu, sd, su, dd, du, rd, ru, zr, zs, base, prow, hacc, part, ar, own_sh, sh, sexp_h, sexp_m, uh,
     seg, mslots, mids, stor, pos, slot_s,
     out_v, in_sem, loc_sem, p1_s, p1_r, g_s, g_r, d_s, d_r, z_s, z_r, a_s, a_r,
 ):
@@ -180,8 +181,8 @@
 
         lax.fori_loop(0, MISS, one, 0, unroll=14)
 
-    def deliver(kind):
-        for o in near_last + (0,):
+    def deliver(kind, offsets=(4, 5, 2, 6, 3, 7, 1, 0)):
+        for o in offsets:
             for mode in range(2):
                 q = member[mode]
                 t = partner(mode, o)
@@ -244,7 +245,7 @@
             start, missed, hit = carry
             is_miss = jnp.logical_and(missed < MISS, mslots[0, jnp.minimum(missed, MISS - 1)] == s)
             slot_s[0, s] = start
-            slot_s[1, s] = jnp.where(is_miss, HITS + missed, hit)
+            slot_s[1, s] = jnp.where(is_miss, FIRST_MISS + missed, hit)
             step = jnp.where(is_miss, 1, 0)
             return start + seg[0, s], missed + step, hit + 1 - step
 
@@ -288,7 +289,7 @@
             )
             xm = lax.dot_general(att[rows, :], miss, NT, preferred_element_type=F32)
             for b in range(7):
-                acc = acc + jnp.where(pm == HITS + 4 * b, xm[:, 128 * b:128 * b + 128], 0.0)
+                acc = acc + jnp.where(pm == FIRST_MISS + 4 * b, xm[:, 128 * b:128 * b + 128], 0.0)
             acc = acc + pltpu.roll(acc, 64, 1)
             acc = acc + pltpu.roll(acc, 32, 1)
             sums.append(acc)
@@ -336,46 +337,53 @@
             pick = row_e == 64 * t + (col_e // 128) * 16 + col_e % 16
             spread = jnp.dot(s, jnp.where(pick, 1.0, 0.0).astype(BF), preferred_element_type=F32)
             pm = prow[rows, :] - lane // 16
-            for b in range(5):
+            for b in range(6):
                 m = pm == 8 * b
                 for rb in range(4):
-                    sexp[rows, 640 * rb + 128 * b:640 * rb + 128 * b + 128] = jnp.where(
-                        m, spread[:, 128 * rb:128 * rb + 128], 0.0
-                    ).astype(BF)
+                    v = jnp.where(m, spread[:, 128 * rb:128 * rb + 128], 0.0).astype(BF)
+                    if b < 2:
+                        sexp_h[rows, 256 * rb + 128 * b:256 * rb + 128 * b + 128] = v
+                    else:
+                        at = 512 * rb + 128 * (b - 2)
+                        sexp_m[rows, at:at + 128] = v
+
+    def up_hits():
+        for rb in range(4):
+            uh[256 * rb:256 * rb + 192, :] = cu[:, 16 * rb:16 * rb + 16, :].reshape(192, CHUNK)
+            uh[256 * rb + 192:256 * rb + 256, :] = jnp.zeros((64, CHUNK), BF)
+
+    def grow_hits(i):
+        rows = slice(256 * i, 256 * i + 256)
+        base[rows, :] += jnp.dot(sexp_h[rows, :], uh[...], preferred_element_type=F32)
+
+    def out_copy(i):
+        rows = pl.ds(256 * i, 256)
+        return pltpu.make_async_copy(out_v.at[rows], out_ref.at[rows], in_sem.at[14 + i])
 
     def grow(i):
         rows = slice(256 * i, 256 * i + 256)
-        acc = base[rows, :]
+        acc = jnp.concatenate(
+            [
+                base[rows, 0:HALF] + zr[0, 6, rows, :].astype(F32) + zr[1, 5, rows, :].astype(F32),
+                base[rows, HALF:] + zr[0, 5, rows, :].astype(F32) + zr[1, 6, rows, :].astype(F32),
+            ],
+            axis=1,
+        )
         for rb in range(4):
             mode, first = rb // 2, (rb % 2) * 4
             up = jnp.concatenate(
                 [
-                    cu[:, 16 * rb:16 * rb + 16, :].reshape(HITS * 16, CHUNK),
                     jnp.concatenate(
                         [ru[mode, first + cb].reshape(MISS * 16, 128) for cb in range(4)], axis=1
                     ),
+                    jnp.zeros((64, CHUNK), BF),
                 ],
                 axis=0,
             )
             acc = acc + jnp.dot(
-                sexp[rows, 640 * rb:640 * rb + 640], up, preferred_element_type=F32
+                sexp_m[rows, 512 * rb:512 * rb + 512], up, preferred_element_type=F32
             )
-        base[rows, :] = acc
-
-    def out_copy(i):
-        rows = pl.ds(256 * i, 256)
-        return pltpu.make_async_copy(out_v.at[rows], out_ref.at[rows], in_sem.at[14 + i])
-
-    def finish(i):
-        rows = slice(256 * i, 256 * i + 256)
-        for half in range(2):
-            cols = slice(HALF * half, HALF * half + HALF)
-            k0 = 6 if half == 0 else 5
-            out_v[rows, cols] = (
-                base[rows, cols]
-                + zr[0, k0, rows, :].astype(F32)
-                + zr[1, 11 - k0, rows, :].astype(F32)
-            ).astype(BF)
+        out_v[rows, :] = acc.astype(BF)
         out_copy(i).start()
 
     def drain():
@@ -413,6 +421,7 @@
     loads[4].wait()
     shrink_hits()
     own_chunk()
+    up_hits()
     gather_wait(0)
     deliver(0)
     gather_forward(1)
@@ -421,25 +430,22 @@
     ring_step(6, 0, 2)
     deliver_wait(0)
     shrink(0)
+    shrink(1)
     gather_wait(1)
     deliver(1)
-    shrink(1)
     shrink(2)
     rank_sums(0)
     rank_sums(1)
     ring_step(6, 2, 3)
     rank_sums(2)
-    expand(0)
+    for i in range(3):
+        expand(i)
+        grow_hits(i)
     deliver_wait(1)
-    grow(0)
-    expand(1)
-    grow(1)
-    expand(2)
-    grow(2)
     await_recv(zr.at[:, 5], z_r.at[5])
     await_recv(zr.at[:, 6], z_r.at[6])
     for i in range(3):
-        finish(i)
+        grow(i)
     drain()
 
 
@@ -473,7 +479,9 @@
             pltpu.VMEM((3, 7, 16, 128), F32),
             pltpu.VMEM((3, 16, 128), BF),
             pltpu.VMEM((3, 128, 128), BF),
-            pltpu.VMEM((ROWS, 2560), BF),
+            pltpu.VMEM((ROWS, 1024), BF),
+            pltpu.VMEM((ROWS, 2048), BF),
+            pltpu.VMEM((1024, CHUNK), BF),
             pltpu.SMEM((1, USED), jnp.int32),
             pltpu.SMEM((1, MISS), jnp.int32),
             pltpu.SMEM((32, MISS), jnp.int32),

time: 86 us -> 84.2 us (0.979)
  Pallas kernels: 83.8 us -> 82 us
    pallas_call x1, Pallas kernels: 83.8 us -> 82 us  [per_device(): pl.pallas_call(kernel, out_shape=jax.ShapeDtypeStruct((ROWS, CHUNK), BF),...]
where the time goes in v4:
time: 84.2 us; the launch traced here: 84.1 us
  Pallas kernels  82 us (97%)
  local copies, waits for them, and re-layouts  2.06 us (2%)
    pallas_call x1, Pallas kernels, per_device(): pl.pallas_call(kernel, out_shape=jax.ShapeDtypeStruct((ROWS, CHUNK), BF),...  82 us
    unnamed x1, local copies, waits for them, and re-layouts  2.06 us

profile of v4, /device:TPU:1, one launch (start us, length us, event | category | flops | bytes accessed | tf_op | source)
XLA Modules:
  0.0 84.1 jit_solution(6811583884568672505)
XLA Ops:
  0.0 82.0 %lora_projection.1 = bf16[768,512]{1,0:T(8,128)(2,1)} custom-call(bf16[768,1024]{1,0:T(8,128)(2,1)} %att_h.1, bf16[1024,4096]{1,0:T(8,128)(2,1)} %w_h.1, bf16[12,64,1024]{2,1,0:T(8,128)(2,1)} %cd_h.1, bf16[12,64,512]{2,1,0:T(8,128)(2,1)} %cu_h.1, bf16[8,64,1024]{2,1,0:T(8,128)(2,1)} %pd_h.1, bf16[8,64,512]{2,1,0:T(8,128)(2,1)} %pu_h.1, s32[1,40]{1,0:T(1,128)} %seg_h.1, ...), custom_call_target="tpu_custom_call" | custom-call | flops 12499999744 | bytes 14000000 | tf_op jit(solution)/shard_map/lora_projection/pallas_call | solution.py:455
  82.0 2.1 %copy.12 = bf16[768,512]{1,0:T(8,128)(2,1)} copy(bf16[768,512]{1,0:T(8,128)(2,1)} %lora_projection.1) | data formatting | bytes 1572864

commit v5 on v4

--- a/solution.py
+++ b/solution.py
@@ -436,8 +436,8 @@
     shrink(2)
     rank_sums(0)
     rank_sums(1)
+    rank_sums(2)
     ring_step(6, 2, 3)
-    rank_sums(2)
     for i in range(3):
         expand(i)
         grow_hits(i)

time: 84.2 us -> 84.2 us (level)
  no operation moved by 1% of the time
where the time goes in v5:
time: 84.2 us; the launch traced here: 84.1 us
  Pallas kernels  82 us (97%)
  local copies, waits for them, and re-layouts  2.06 us (2%)
    pallas_call x1, Pallas kernels, per_device(): pl.pallas_call(kernel, out_shape=jax.ShapeDtypeStruct((ROWS, CHUNK), BF),...  82 us
    unnamed x1, local copies, waits for them, and re-layouts  2.06 us

profile of v5, /device:TPU:1, one launch (start us, length us, event | category | flops | bytes accessed | tf_op | source)
XLA Modules:
  0.0 84.1 jit_solution(320979665407763338)
XLA Ops:
  0.0 82.0 %lora_projection.1 = bf16[768,512]{1,0:T(8,128)(2,1)} custom-call(bf16[768,1024]{1,0:T(8,128)(2,1)} %att_h.1, bf16[1024,4096]{1,0:T(8,128)(2,1)} %w_h.1, bf16[12,64,1024]{2,1,0:T(8,128)(2,1)} %cd_h.1, bf16[12,64,512]{2,1,0:T(8,128)(2,1)} %cu_h.1, bf16[8,64,1024]{2,1,0:T(8,128)(2,1)} %pd_h.1, bf16[8,64,512]{2,1,0:T(8,128)(2,1)} %pu_h.1, s32[1,40]{1,0:T(1,128)} %seg_h.1, ...), custom_call_target="tpu_custom_call" | custom-call | flops 12499999744 | bytes 14000000 | tf_op jit(solution)/shard_map/lora_projection/pallas_call | solution.py:455
  82.0 2.1 %copy.12 = bf16[768,512]{1,0:T(8,128)(2,1)} copy(bf16[768,512]{1,0:T(8,128)(2,1)} %lora_projection.1) | data formatting | bytes 1572864
